TPU v7x, 512 devices: a whole 4x4x16 slice. The times are simulated.
512 devices in a mesh: partitio: 64 (over z, y), snapshot: 8 (over x, core).
Axes of the slice: x: 4, y: 4, z: 16, core: 2. Of those that a mesh axis runs over, the one named last changes fastest.
Arguments:
- snapshots: float32 [256, 65536], P('snapshot', 'partitio'), may hold values from -50 to 50
- connect: int32 [4, 327680], P(None, 'partitio'), may hold values from 0 to 1023
- elem_mask: int32 [327680], P('partitio'), may hold values from 0 to 1, as said below
- volume: float32 [327680], P('partitio'), may hold values from 0.5 to 4
- owned: int32 [65536], P('partitio'), may hold values 0 or 1
- peer_ids: int32 [64, 4], P('partitio'), may hold values from 0 to 63, as said below
- peer_back: int32 [64, 4], P('partitio'), may hold values from 0 to 3, as said below
- iface_rows: int32 [64, 4, 128], P('partitio'), may hold values from 0 to 1023
- iface_mask: int32 [64, 4, 128], P('partitio'), may hold values from 0 to 1, as said below
Outputs:
- mass_snap: float32 [256, 65536], P('snapshot', 'partitio')
- gram_matrix: float32 [256, 256], P(None, 'partitio')
Inputs may be any that keep to these rules, and one draw needn't show every extreme that they name: Each partition's 4 peers are distinct partitions other than itself; q is a peer of p exactly when p is a peer of q, and peer_ids[q, peer_back[p, k]] = p for q = peer_ids[p, k]. `peer_back`: see peer_ids. `iface_mask`: the used slots of each list come first; the list of p for peer q and the list of q for p have the same number of used slots, and slot j of one is the same global node as slot j of the other; at least 32 slots of every list are used and some list uses all 128. `elem_mask`: in each aligned block of 128 element slots the real elements come first, 64 or more of them.
All inputs are finite; a program needn't handle non-finite values. No bound on the sum of `owned` on one device may be relied on, other than what follows from the above.
Results may differ from a plain program's by a relative error of at most 0.000075.
Values sent between devices are 32-bit elements; how exact they have to be, the bound alone decides.
No kernel may reach another device: no remote copies, remote signals or barrier semaphores. Data moves between devices by JAX's collectives and lax.ppermute only.
A program may use at most 64 MiB of HBM per device.

v0:
```python
import jax
import jax.numpy as jnp
from jax import lax
from jax.sharding import PartitionSpec as P


def per_device(
    snapshots, connect, elem_mask, volume, owned, peer_ids, peer_back, iface_rows, iface_mask
):
    snap_count, node_count = snapshots.shape
    weight = volume * (elem_mask.astype(jnp.float32) * 0.05)
    mass_part = jnp.zeros_like(snapshots)
    for block_index in range(connect.shape[1] // node_count):
        first_elem = block_index * node_count
        conn_block = connect[:, first_elem : first_elem + node_count]
        values = snapshots[:, conn_block]
        elem_sum = jnp.sum(values, axis=1, keepdims=True)
        contrib = (values + elem_sum) * weight[None, None, first_elem : first_elem + node_count]
        mass_part = mass_part.at[:, conn_block.reshape(-1)].add(contrib.reshape(snap_count, -1))
    send_rows = jnp.take(mass_part, iface_rows[0], axis=1)
    peer_count = iface_rows.shape[1]
    gathered = lax.all_gather(send_rows, "partitio", axis=1, tiled=True)
    source_index = peer_ids[0] * peer_count + peer_back[0]
    received = jnp.take(gathered, source_index, axis=1)
    live_slots = iface_mask[0].astype(jnp.float32)
    mass_snap = mass_part.at[:, iface_rows[0].reshape(-1)].add(
        (received * live_slots[None]).reshape(snap_count, -1)
    )
    owned_snap = snapshots * owned.astype(jnp.float32)[None, :]
    partial_value = lax.dot_general(
        owned_snap,
        lax.all_gather(mass_snap, "snapshot", axis=0, tiled=True),
        (((1,), (1,)), ((), ())),
        precision=lax.Precision.HIGHEST,
        preferred_element_type=jnp.float32,
    )
    tile_block = lax.psum_scatter(partial_value, "partitio", scatter_dimension=1, tiled=True)
    gram_cols = lax.all_gather(tile_block, "snapshot", axis=0, tiled=True)
    return (mass_snap, gram_cols / (lax.axis_size("partitio") * node_count))


def solution(mesh):
    in_specs = (
        P("snapshot", "partitio"),
        P(None, "partitio"),
        P("partitio"),
        P("partitio"),
        P("partitio"),
        P("partitio", None),
        P("partitio", None),
        P("partitio", None, None),
        P("partitio", None, None),
    )
    out_specs = (P("snapshot", "partitio"), P(None, "partitio"))
    return jax.shard_map(
        per_device, mesh=mesh, in_specs=in_specs, out_specs=out_specs, check_vma=False
    )
```

profile of v0, /device:TPU:1, one launch (start us, length us, event | category | flops | bytes accessed | tf_op | source)
XLA Modules:
  0.0 683.9 jit_solution(10545782807514063463)
XLA Ops:
  7.2 0.0 all-gather.4.cloned.1.call-start
  7.2 0.7 fusion.21
  7.9 0.7 compare_and_fusion
  8.6 0.8 fusion.20
  9.5 1.1 copy.44
  10.6 10.8 %gather_fusion = f32[4096,32]{1,0:T(8,128)S(1)} fusion(f32[32,1024]{0,1:T(8,128)S(1)} %copy.44, s32[4096]{0:T(1024)S(1)} %bitcast_clamp_fusion.4), kind=kCustom, calls=%fused_computation | custom fusion | bytes 1064960 | tf_op jit(solution)/shard_map/gather | solution.py:16
  21.4 0.2 reduce_sum.45
  21.5 0.0 copy-start.6
  21.6 0.0 copy-start.7
  21.6 1.5 broadcast_add_fusion.4
  23.1 0.0 copy-done.6
  23.1 0.0 copy-done.7
  23.2 10.8 %gather_fusion.1 = f32[4096,32]{1,0:T(8,128)S(1)} fusion(f32[32,1024]{0,1:T(8,128)S(1)} %copy.44, s32[4096]{0:T(1024)S(1)} %get-tuple-element.30), kind=kCustom, calls=%fused_computation.1 | custom fusion | bytes 1064960 | tf_op jit(solution)/shard_map/gather | solution.py:16
  34.0 0.2 reduce_sum.46
  34.2 1.5 broadcast_add_fusion.3
  35.8 10.8 %gather_fusion.2 = f32[4096,32]{1,0:T(8,128)S(1)} fusion(f32[32,1024]{0,1:T(8,128)S(1)} %copy.44, s32[4096]{0:T(1024)S(1)} %get-tuple-element.29), kind=kCustom, calls=%fused_computation.2 | custom fusion | bytes 1064960 | tf_op jit(solution)/shard_map/gather | solution.py:16
  46.5 0.2 reduce_sum.47
  46.7 1.5 broadcast_add_fusion.2
  48.3 10.8 %gather_fusion.3 = f32[4096,32]{1,0:T(8,128)S(1)} fusion(f32[32,1024]{0,1:T(8,128)S(1)} %copy.44, s32[4096]{0:T(1024)S(1)} %get-tuple-element.28), kind=kCustom, calls=%fused_computation.3 | custom fusion | bytes 1064960 | tf_op jit(solution)/shard_map/gather | solution.py:16
  59.1 0.2 reduce_sum.48
  59.2 1.4 broadcast_add_fusion.1
  60.8 10.8 %gather_fusion.4 = f32[4096,32]{1,0:T(8,128)S(1)} fusion(f32[32,1024]{0,1:T(8,128)S(1)} %copy.44, s32[4096]{0:T(1024)S(1)} %get-tuple-element.27), kind=kCustom, calls=%fused_computation.4 | custom fusion | bytes 1064960 | tf_op jit(solution)/shard_map/gather | solution.py:16
  71.5 0.2 reduce_sum.49
  71.7 0.0 copy-start
  71.7 1.5 broadcast_add_fusion
  73.2 0.8 copy-done
  74.1 2.0 bitcast_multiply_fusion.4
  76.1 20.9 %scatter_custom_fusion = f32[32,1024]{0,1:T(8,128)S(1)} fusion(s32[4096]{0:T(1024)S(1)} %bitcast.178, f32[32,4096]{0,1:T(8,128)} %bitcast_multiply_fusion.4, f32[]{:T(128)} %constant.13.clone.1), kind=kCustom, calls=%fused_computation.25 | custom fusion | flops 131072 | bytes 655364 | tf_op jit(solution)/shard_map/scatter-add | solution.py:19
  97.0 0.0 copy-done.1
  97.0 0.0 copy-start.2
  97.0 2.0 bitcast_multiply_fusion.3
  99.0 0.0 copy-done.2
  99.0 1.9 bitcast_multiply_fusion.2
  100.9 1.9 bitcast_multiply_fusion.1
  102.9 0.6 bitcast_multiply_fusion
  103.5 23.0 %scatter_custom_fusion.1 = f32[32,1024]{0,1:T(8,128)S(1)} fusion(f32[32,1024]{0,1:T(8,128)S(1)} %scatter_custom_fusion, s32[4096]{0:T(1024)S(1)} %bitcast.179, f32[32,4096]{0,1:T(8,128)} %bitcast_multiply_fusion.3), kind=kCustom, calls=%fused_computation.22 | custom fusion | flops 131072 | bytes 655360 | tf_op jit(solution)/shard_map/scatter-add | solution.py:19
  126.5 23.0 %scatter_custom_fusion.2 = f32[32,1024]{0,1:T(8,128)S(1)} fusion(f32[32,1024]{0,1:T(8,128)S(1)} %scatter_custom_fusion.1, s32[4096]{0:T(1024)S(1)} %bitcast.180, f32[32,4096]{0,1:T(8,128)} %bitcast_multiply_fusion.2), kind=kCustom, calls=%fused_computation.19 | custom fusion | flops 131072 | bytes 655360 | tf_op jit(solution)/shard_map/scatter-add | solution.py:19
  149.5 23.2 %scatter_custom_fusion.3 = f32[32,1024]{0,1:T(8,128)S(1)} fusion(f32[32,1024]{0,1:T(8,128)S(1)} %scatter_custom_fusion.2, s32[4096]{0:T(1024)S(1)} %bitcast.181, f32[32,4096]{0,1:T(8,128)} %bitcast_multiply_fusion.1), kind=kCustom, calls=%fused_computation.16 | custom fusion | flops 131072 | bytes 655360 | tf_op jit(solution)/shard_map/scatter-add | solution.py:19
  172.7 0.0 copy-start.11
  172.7 0.0 copy-start.12
  172.7 0.0 copy-start.8
  172.8 0.0 copy-start.10
  172.8 22.6 %scatter_custom_fusion.4 = f32[32,1024]{0,1:T(8,128)S(1)} fusion(f32[32,1024]{0,1:T(8,128)S(1)} %scatter_custom_fusion.3, s32[4096]{0:T(1024)S(1)} %bitcast.182, f32[32,4096]{0,1:T(8,128)S(1)} %bitcast_multiply_fusion), kind=kCustom, calls=%fused_computation.13 | custom fusion | flops 131072 | bytes 2228224 | tf_op jit(solution)/shard_map/scatter-add | solution.py:19
  195.4 0.0 copy-start.9
  195.4 0.0 copy-start.5
  195.4 1.0 gather_fusion.5
  196.5 0.1 copy.49
  196.6 0.6 select_bitcast_fusion
  197.2 0.0 all-gather.4.cloned.1.call-update
  197.2 0.0 all-gather.6.cloned.1.call-start
  197.3 0.1 broadcast_bitcast_fusion.5
  197.4 143.7 %all-gather.4.cloned.1.call-done = f32[32,256,128]{2,0,1:T(8,128)} async-done(((f32[32,4,128]{2,0,1:T(8,128)}), f32[32,256,128]{2,0,1:T(8,128)}) %all-gather.4.cloned.1.call-update) | async-done | bytes 4194320 | tf_op jit(solution)/shard_map/all_gather | solution.py:22
  341.2 2.7 gather_fusion.6
  344.0 0.1 copy.51
  344.1 3.5 scatter_fusion
  347.6 0.8 copy.54
  348.4 0.0 all-gather.6.cloned.1.call-update
  348.5 1.3 dynamic-slice
  350.4 32.5 %all-gather.6.cloned.1.call-done = f32[256,1024]{1,0:T(8,128)} async-done(((f32[32,1024]{1,0:T(8,128)}), f32[256,1024]{1,0:T(8,128)}) %all-gather.6.cloned.1.call-update) | async-done | bytes 1048592 | tf_op jit(solution)/shard_map/all_gather | solution.py:32
  382.9 0.0 copy-done.5
  382.9 2.2 fusion.11
  385.1 225.3 %all-reduce = f32[32,256]{0,1:T(8,128)S(1)} all-reduce(f32[32,256]{0,1:T(8,128)S(1)} %fusion.11), channel_id=2, replica_groups=mesh['partitio'=64,'snapshot'=8] {'partitio'}, use_global_device_ids=true, to_apply=%region_11.12.clone | all-reduce | flops 8192 | bytes 65536
  610.4 66.0 %all-gather = f32[8,32,4]{1,2,0:T(4,128)S(1)} all-gather(f32[1,32,4]{1,2,0:T(4,128)S(1)} %dynamic-slice_bitcast_fusion), channel_id=1, replica_groups=mesh['partitio'=64,'snapshot'=8] {'snapshot'}, dimensions={0}, use_global_device_ids=true | all-gather | bytes 4608 | tf_op jit(solution)/shard_map/all_gather | solution.py:38
  676.4 0.7 reshape.428
  (43 shorter events, 0.3 us)
Async XLA Ops:
  7.2 334.0 %all-gather.4.cloned.1.call-start = ((), (), s32[]{:S(2)}) async-start(), calls=%async_computation | async-start | bytes 4259840 | tf_op jit(solution)/shard_map/all_gather | solution.py:22
  21.5 1.6 copy-start.6
  21.6 1.6 copy-start.7
  71.7 2.3 copy-start
  76.1 21.0 %copy-start.1 = (f32[32,4,1024]{0,2,1:T(8,128)S(1)}, f32[32,4,1024]{0,2,1:T(8,128)}, u32[]{:S(2)}) copy-start(f32[32,4,1024]{0,2,1:T(8,128)} %broadcast_add_fusion.3) | copy-start | bytes 1572868
  97.0 2.0 copy-start.2
  99.0 1.9 copy-start.3
  100.9 1.9 copy-start.4
  172.7 24.6 %copy-start.11 = (s32[1,4]{1,0:T(1,128)S(1)}, s32[1,4]{1,0:T(1,128)}, u32[]{:S(2)}) copy-start(s32[1,4]{1,0:T(1,128)} %param.15) | copy-start | bytes 52
  172.7 24.6 %copy-start.12 = (s32[1,4]{1,0:T(1,128)S(1)}, s32[1,4]{1,0:T(1,128)}, u32[]{:S(2)}) copy-start(s32[1,4]{1,0:T(1,128)} %param.14) | copy-start | bytes 52
  172.7 24.7 %copy-start.8 = (s32[1,4,128]{2,1,0:T(4,128)S(1)}, s32[1,4,128]{2,1,0:T(4,128)}, u32[]{:S(2)}) copy-start(s32[1,4,128]{2,1,0:T(4,128)} %param.16) | copy-start | bytes 6148
  172.8 24.7 %copy-start.10 = (s32[1,4,128]{2,1,0:T(4,128)S(1)}, s32[1,4,128]{2,1,0:T(4,128)}, u32[]{:S(2)}) copy-start(s32[1,4,128]{2,1,0:T(4,128)} %param.17) | copy-start | bytes 6148
  195.4 153.1 %copy-start.9 = (s32[1024]{0:T(1024)S(1)}, s32[1024]{0:T(1024)}, u32[]{:S(2)}) copy-start(s32[1024]{0:T(1024)} %param.13) | copy-start | bytes 12292
  195.4 187.5 %copy-start.5 = (f32[32,1024]{1,0:T(8,128)S(1)}, f32[32,1024]{1,0:T(8,128)}, u32[]{:S(2)}) copy-start(f32[32,1024]{1,0:T(8,128)} %param.9) | copy-start | bytes 393220
  197.2 185.7 %all-gather.6.cloned.1.call-start = ((), (), s32[]{:S(2)}) async-start(), calls=%async_computation.1 | async-start | bytes 1179648 | tf_op jit(solution)/shard_map/all_gather | solution.py:32
Sparse Core Ops, SparseCore 0:
  197.4 143.7 all-gather.3
  348.6 34.2 all-gather.5
where the time goes:
time: 684 us
  blocking collectives  291 us (43%)
  waiting for transfers between devices  176 us (26%)
  other arithmetic  136 us (20%)
  local copies, waits for them, and re-layouts  62.8 us (9%)
  between operations  15.2 us (2%)
    unnamed x1, blocking collectives  225 us
    all_gather x1, waiting for transfers between devices, per_device(): gathered = lax.all_gather(send_rows, 'partitio', axis=1, tiled=True)  144 us
    scatter-add x5, other arithmetic, per_device(): mass_part.at[:, conn_block.reshape(-1)].add(contrib.reshape(snap_count, -1))  113 us
    all_gather x1, blocking collectives, per_device(): gram_cols = lax.all_gather(tile_block, 'snapshot', axis=0, tiled=True)  66 us
    gather x5, local copies, waits for them, and re-layouts, per_device(): values = snapshots[:, conn_block]  53.9 us
    all_gather x1, waiting for transfers between devices, per_device(): lax.all_gather(mass_snap, 'snapshot', axis=0, tiled=True)  32.5 us
  transfers between devices with their start and end apart: 2, of which 2 were waited for; matrix products, arithmetic and copies ran while one was open for 0% of the time, Pallas kernels for 0%

commit v1 on v0

v1 whole, which is shorter than its diff:
```python
import jax
import jax.numpy as jnp
from jax import lax
from jax.experimental import pallas as pl
from jax.experimental.pallas import tpu as pltpu
from jax.sharding import Mesh, PartitionSpec as P

F32 = jnp.float32
BF16 = jnp.bfloat16
NT = (((1,), (1,)), ((), ()))
CHUNK = 512
LANES = 128


def split2(x):
    high = x.astype(BF16)
    low = (x - high.astype(F32)).astype(BF16)
    return jnp.concatenate([high, low], axis=0)


def one_hot_block(lists, first, rows):
    iota = lax.broadcasted_iota(jnp.int32, (rows, lists[0].shape[1]), 0).astype(F32).astype(BF16)
    count = None
    for entry in lists:
        near = (entry - first).astype(F32).astype(BF16)
        hit = jnp.where(iota == near, jnp.ones((), BF16), jnp.zeros((), BF16))
        count = hit if count is None else count + hit
    return count


def fill_one_hot(ref, lists):
    for first in range(0, ref.shape[0], 256):
        ref[first : first + 256, :] = one_hot_block(lists, first, 256)


def local_kernel(peer_ref, snap_ref, conn_ref, mask_ref, vol_ref, rows_ref, mass_ref, send_ref, hot_ref, acc_ref, slot_ref):
    snaps = snap_ref.shape[0]
    snap = snap_ref[...]
    snap2 = split2(snap)
    acc_ref[...] = jnp.zeros_like(acc_ref)
    for step in range(conn_ref.shape[1] // CHUNK):
        cols = slice(step * CHUNK, (step + 1) * CHUNK)
        hot = hot_ref.at[step % 2]
        fill_one_hot(hot, [conn_ref[i : i + 1, cols] for i in range(4)])
        weight = vol_ref[:, cols] * (mask_ref[:, cols].astype(F32) * 0.05)
        both = jnp.dot(snap2, hot[...], preferred_element_type=F32)
        value = (both[:snaps] + both[snaps:]) * weight
        weight2 = split2(jnp.broadcast_to(weight, (8, CHUNK)))
        left = jnp.concatenate([split2(value), weight2], axis=0)
        acc_ref[...] += lax.dot_general(left, hot[...], NT, preferred_element_type=F32)
    diag = acc_ref[2 * snaps : 2 * snaps + 1] + acc_ref[2 * snaps + 8 : 2 * snaps + 9]
    mass = acc_ref[:snaps] + acc_ref[snaps : 2 * snaps] + snap * diag
    mass_ref[...] = mass
    fill_one_hot(slot_ref, [jnp.concatenate([rows_ref[k : k + 1, :] for k in range(4)], axis=1)])
    both = jnp.dot(split2(mass), slot_ref[...], preferred_element_type=F32)
    picked = both[:snaps] + both[snaps:]
    send_ref[...] = jnp.zeros_like(send_ref)
    for k in range(4):
        send_ref[peer_ref[0, k]] = picked[:, k * LANES : (k + 1) * LANES]


def final_kernel(peer_ref, recv_ref, rows_ref, live_ref, mass_ref, all_ref, owned_ref, out_ref, gram_ref, slot_ref):
    snaps = mass_ref.shape[0]
    parts = []
    for k in range(4):
        live = live_ref[k : k + 1, :].astype(F32)
        parts.append(recv_ref[peer_ref[0, k]] * live)
    fill_one_hot(slot_ref, [jnp.concatenate([rows_ref[k : k + 1, :] for k in range(4)], axis=1)])
    added = lax.dot_general(split2(jnp.concatenate(parts, axis=1)), slot_ref[...], NT, preferred_element_type=F32)
    total = mass_ref[...] + (added[:snaps] + added[snaps:])
    out_ref[...] = total
    left = split2(all_ref[...] * owned_ref[...].astype(F32))
    both = lax.dot_general(split2(total), left, NT, preferred_element_type=F32)
    count = all_ref.shape[0]
    gram_ref[...] = (
        both[:snaps, :count] + (both[snaps:, :count] + both[:snaps, count:])
    )


def vmem(count):
    return [pl.BlockSpec(memory_space=pltpu.VMEM)] * count


def per_device(snapshots, connect, elem_mask, volume, owned, peer_ids, peer_back, iface_rows, iface_mask):
    snaps, nodes = snapshots.shape
    zs, ys = lax.axis_size("z"), lax.axis_size("y")
    groups = lax.axis_size("x") * lax.axis_size("core")
    parts = zs * ys
    params = pltpu.CompilerParams(vmem_limit_bytes=40 * 1024 * 1024)
    smem = pl.BlockSpec(memory_space=pltpu.SMEM)
    all_snaps = lax.all_gather(snapshots, ("x", "core"), axis=0, tiled=True)
    mass, send = pl.pallas_call(
        local_kernel,
        out_shape=(
            jax.ShapeDtypeStruct((snaps, nodes), F32),
            jax.ShapeDtypeStruct((parts, snaps, LANES), F32),
        ),
        in_specs=[smem] + vmem(5),
        out_specs=tuple(vmem(2)),
        scratch_shapes=[
            pltpu.VMEM((2, nodes, CHUNK), BF16),
            pltpu.VMEM((2 * snaps + 16, nodes), F32),
            pltpu.VMEM((nodes, 4 * LANES), BF16),
        ],
        compiler_params=params,
        name="local_mass",
    )(peer_ids, snapshots, connect, elem_mask[None], volume[None], iface_rows[0])
    recv = lax.all_to_all(send, ("z", "y"), 0, 0, tiled=True)
    mass_snap, gram = pl.pallas_call(
        final_kernel,
        out_shape=(
            jax.ShapeDtypeStruct((snaps, nodes), F32),
            jax.ShapeDtypeStruct((snaps, snaps * groups), F32),
        ),
        in_specs=[smem] + vmem(6),
        out_specs=tuple(vmem(2)),
        scratch_shapes=[pltpu.VMEM((nodes, 4 * LANES), BF16)],
        compiler_params=params,
        name="assemble_gram",
    )(peer_ids, recv, iface_rows[0], iface_mask[0], mass, all_snaps, owned[None])
    gram = gram * (1.0 / (parts * nodes))
    per_z = snaps // (ys * 4)
    gram = gram.reshape(per_z, ys, 4, groups, snaps).transpose(1, 3, 0, 2, 4)
    gram = lax.all_to_all(gram.reshape(ys * groups, per_z * 4 * snaps), ("y", "x", "core"), 0, 0, tiled=True)
    gram = jnp.sum(gram.reshape(ys, zs, 4 * snaps), axis=0)
    gram = lax.all_to_all(gram, "z", 0, 0, tiled=True)
    gram = jnp.sum(gram.reshape(zs, 1, 4 * snaps), axis=0)
    gram = lax.all_to_all(jnp.broadcast_to(gram, (groups, 4 * snaps)), ("x", "core"), 0, 0, tiled=True)
    gram = gram.reshape(groups, 4, snaps).transpose(0, 2, 1).reshape(groups * snaps, 4)
    return mass_snap, gram


def solution(mesh):
    sizes = (16, 4, 4, 2)
    fine = Mesh(mesh.devices.reshape(sizes), ("z", "y", "x", "core"))
    part, snap = ("z", "y"), ("x", "core")
    in_specs = (
        P(snap, part),
        P(None, part),
        P(part),
        P(part),
        P(part),
        P(part, None),
        P(part, None),
        P(part, None, None),
        P(part, None, None),
    )
    out_specs = (P(snap, part), P(None, part))
    return jax.shard_map(per_device, mesh=fine, in_specs=in_specs, out_specs=out_specs, check_vma=False)
```

time: 684 us -> 145 us (0.21)
  blocking collectives: 291 us -> 40.9 us
  other arithmetic: 136 us -> 0.7 us
  waiting for transfers between devices: 176 us -> 51.4 us
  local copies, waits for them, and re-layouts: 62.8 us -> 6.69 us
  starting transfers between devices: 0.08 us -> 19.3 us
  Pallas kernels: 0 us -> 11.5 us
    unnamed x1 -> x0, blocking collectives: 225 us -> none
    all_gather x2 -> x1, waiting for transfers between devices: 176 us -> 34.8 us  [per_device(): all_snaps = lax.all_gather(snapshots, ('x', 'core'), axis=0, tiled=True)]
    scatter-add x6 -> x0, other arithmetic: 116 us -> none  [the longest x5 113 us: per_device(): mass_part.at[:, conn_block.reshape(-1)].add(contrib.reshape(snap_count, -1))]
    all_gather x1 -> x0, blocking collectives: 66 us -> none  [per_device(): gram_cols = lax.all_gather(tile_block, 'snapshot', axis=0, tiled=True)]
    gather x8 -> x0, local copies, waits for them, and re-layouts: 57.7 us -> none  [the longest x5 53.9 us: per_device(): values = snapshots[:, conn_block]]
    all_to_all x0 -> x3, blocking collectives: none -> 40.9 us  [the longest x1 18.7 us: per_device(): lax.all_to_all(gram.reshape(ys * groups, per_z * 4 * snaps), ('y', 'x', '...]
    all_to_all x0 -> x1, starting transfers between devices: none -> 19.3 us  [per_device(): recv = lax.all_to_all(send, ('z', 'y'), 0, 0, tiled=True)]
    all_to_all x0 -> x1, waiting for transfers between devices: none -> 15.9 us  [per_device(): recv = lax.all_to_all(send, ('z', 'y'), 0, 0, tiled=True)]
where the time goes in v1:
time: 145 us
  waiting for transfers between devices  51.4 us (35%)
  blocking collectives  40.9 us (28%)
  starting transfers between devices  19.3 us (13%)
  between operations  14.1 us (10%)
  Pallas kernels  11.5 us (8%)
  local copies, waits for them, and re-layouts  6.69 us (5%)
    all_gather x1, waiting for transfers between devices, per_device(): all_snaps = lax.all_gather(snapshots, ('x', 'core'), axis=0, tiled=True)  34.8 us
    all_to_all x1, starting transfers between devices, per_device(): recv = lax.all_to_all(send, ('z', 'y'), 0, 0, tiled=True)  19.3 us
    all_to_all x1, blocking collectives, per_device(): lax.all_to_all(gram.reshape(ys * groups, per_z * 4 * snaps), ('y', 'x', '...  18.7 us
    all_to_all x1, waiting for transfers between devices, per_device(): recv = lax.all_to_all(send, ('z', 'y'), 0, 0, tiled=True)  15.9 us
    all_to_all x1, blocking collectives, per_device(): gram = lax.all_to_all(gram, 'z', 0, 0, tiled=True)  13.8 us
    pallas_call x1, Pallas kernels, per_device(): pl.pallas_call(local_kernel, out_shape=(jax.ShapeDtypeStruct((snaps, node...  9.59 us
    all_to_all x1, blocking collectives, per_device(): lax.all_to_all(jnp.broadcast_to(gram, (groups, 4 * snaps)), ('x', 'core')...  8.42 us
    unnamed x18, local copies, waits for them, and re-layouts  5.15 us
  transfers between devices with their start and end apart: 2, of which 2 were waited for; matrix products, arithmetic and copies ran while one was open for 0% of the time, Pallas kernels for 0%

profile of v1, /device:TPU:1, one launch (start us, length us, event | category | flops | bytes accessed | tf_op | source)
XLA Modules:
  0.0 144.6 jit_solution(5765336048606322385)
XLA Ops:
  7.2 0.0 copy-start.5
  7.2 0.0 copy-start.8
  7.2 0.7 copy-done.5
  7.8 0.0 copy-done.8
  7.9 0.0 copy-start.1
  7.9 0.9 copy-done.1
  8.8 0.0 copy-start.2
  8.8 0.9 copy-done.2
  9.6 0.0 copy-start.3
  9.6 0.7 copy-done.3
  10.4 0.0 copy-start.4
  10.4 0.7 copy-done.4
  11.1 9.6 %local_mass.1 = (f32[32,1024]{1,0:T(8,128)S(1)}, f32[64,32,128]{2,1,0:T(8,128)}) custom-call(s32[1,4]{1,0:T(1,128)S(1)} %copy-done.8, f32[32,1024]{1,0:T(8,128)S(1)} %copy-done.1, s32[4,5120]{1,0:T(4,128)S(1)} %copy-done.2, s32[1,5120]{1,0:T(1,128)S(1)} %bitcast.15, f32[1,5120]{1,0:T(1,128)S(1)} %bitcast.16, s32[4,128]{1,0:T(4,128)S(1)} %bitcast.17), custom_call_target="tpu_custom_call" | custom-call | tf_op jit(solution)/shard_map/local_mass/pallas_call | solution.py:92
  20.7 19.3 %all-to-all-start = ((f32[64,32,128]{2,1,0:T(8,128)}), f32[64,32,128]{2,1,0:T(8,128)S(1)}, u32[]{:S(2)}, u32[]{:S(2)}) async-start(f32[64,32,128]{2,1,0:T(8,128)} %get-tuple-element.6), calls=%async_computation | async-start | bytes 2097152 | tf_op jit(solution)/shard_map/all_to_all | solution.py:108
  40.0 0.0 all-gather.2.cloned.1.call-start
  40.0 0.0 copy-start.7
  40.0 0.7 all-gather.2.cloned.1.call-update
  40.7 0.0 copy-start.6
  40.7 34.8 %all-gather.2.cloned.1.call-done.all_ref = f32[256,1024]{1,0:T(8,128)} async-done(((f32[32,1024]{1,0:T(8,128)}), f32[256,1024]{1,0:T(8,128)}) %all-gather.2.cloned.1.call-update) | async-done | bytes 1048592 | tf_op jit(solution)/shard_map/all_gather | solution.py:91
  75.5 15.9 %all-to-all-done.recv_ref = f32[64,32,128]{2,1,0:T(8,128)S(1)} async-done(((f32[64,32,128]{2,1,0:T(8,128)}), f32[64,32,128]{2,1,0:T(8,128)S(1)}, u32[]{:S(2)}, u32[]{:S(2)}) %all-to-all-start) | async-done | bytes 1048608 | tf_op jit(solution)/shard_map/all_to_all | solution.py:108
  91.4 0.0 copy-done.7
  91.4 0.0 copy-done.6
  91.4 0.0 copy-start
  91.4 1.2 copy-done
  92.6 1.9 %assemble_gram.1 = (f32[32,1024]{1,0:T(8,128)}, f32[32,256]{1,0:T(8,128)S(1)}) custom-call(s32[1,4]{1,0:T(1,128)S(1)} %copy-done.8, f32[64,32,128]{2,1,0:T(8,128)S(1)} %all-to-all-done.recv_ref, s32[4,128]{1,0:T(4,128)S(1)} %bitcast.18, s32[4,128]{1,0:T(4,128)S(1)} %bitcast.20, f32[32,1024]{1,0:T(8,128)S(1)} %get-tuple-element.7.mass_ref, ...), custom_call_target="tpu_custom_call" | custom-call | tf_op jit(solution)/shard_map/assemble_gram/pallas_call | solution.py:109
  94.6 0.1 reshape.32
  94.7 0.1 all_to_all.25
  94.8 18.7 %all_to_all.30 = f32[32,1,256]{2,1,0:T(1,128)S(1)} all-to-all(f32[32,1,256]{2,1,0:T(1,128)S(1)} %all_to_all.25), channel_id=1, replica_groups=mesh['z'=16,'y'=4,'x'=4,'core'=2] {'y','x','core'}, dimensions={0} | all-to-all | bytes 65536 | tf_op jit(solution)/shard_map/all_to_all | solution.py:124
  113.6 13.8 %all_to_all.31 = f32[16,1,128]{2,1,0:T(1,128)S(1)} all-to-all(f32[16,1,128]{2,1,0:T(1,128)S(1)} %bitcast.24), channel_id=1, replica_groups=mesh['z'=16,'y'=4,'x'=4,'core'=2] {'z'}, dimensions={0} | all-to-all | bytes 16384 | tf_op jit(solution)/shard_map/all_to_all | solution.py:126
  127.4 8.4 %all_to_all.32 = f32[8,1,128]{2,1,0:T(1,128)S(1)} all-to-all(f32[8,1,128]{2,1,0:T(1,128)S(1)} %broadcast_in_dim.17), channel_id=1, replica_groups=mesh['z'=16,'y'=4,'x'=4,'core'=2] {'x','core'}, dimensions={0} | all-to-all | bytes 8192 | tf_op jit(solution)/shard_map/all_to_all | solution.py:128
  135.8 0.5 broadcast.6
  136.4 0.7 reduce.6
  137.0 0.1 reshape.34
  137.1 0.7 reshape.35
  (6 shorter events, 0.1 us)
Async XLA Ops:
  7.2 0.7 copy-start.5
  7.2 0.7 copy-start.8
  7.9 0.9 copy-start.1
  8.8 0.9 copy-start.2
  9.6 0.7 copy-start.3
  10.4 0.7 copy-start.4
  20.7 70.7 %all-to-all-start = ((f32[64,32,128]{2,1,0:T(8,128)}), f32[64,32,128]{2,1,0:T(8,128)S(1)}, u32[]{:S(2)}, u32[]{:S(2)}) async-start(f32[64,32,128]{2,1,0:T(8,128)} %get-tuple-element.6), calls=%async_computation | async-start | bytes 2097152 | tf_op jit(solution)/shard_map/all_to_all | solution.py:108
  40.0 35.6 %all-gather.2.cloned.1.call-start = ((), (), s32[]{:S(2)}) async-start(), calls=%async_computation.4 | async-start | bytes 1179648 | tf_op jit(solution)/shard_map/all_gather | solution.py:91
  40.0 51.4 %copy-start.7 = (s32[1,4,128]{2,1,0:T(4,128)S(1)}, s32[1,4,128]{2,1,0:T(4,128)}, u32[]{:S(2)}) copy-start(s32[1,4,128]{2,1,0:T(4,128)} %param.16) | copy-start | bytes 6148
  40.7 50.7 %copy-start.6 = (s32[1024]{0:T(1024)S(1)}, s32[1024]{0:T(1024)}, u32[]{:S(2)}) copy-start(s32[1024]{0:T(1024)} %param.13) | copy-start | bytes 12292
  91.4 1.2 copy-start
Sparse Core Ops, SparseCore 0:
  43.0 32.5 all-gather.1

commit v2 on v1

v2 whole, which is shorter than its diff:
```python
import jax
import jax.numpy as jnp
from jax import lax
from jax.experimental import pallas as pl
from jax.experimental.pallas import tpu as pltpu
from jax.sharding import Mesh, PartitionSpec as P

F32 = jnp.float32
BF16 = jnp.bfloat16
NT = (((1,), (1,)), ((), ()))
CHUNK = 512
LANES = 128
SLOTS = 4
OVERFLOW = 1e30


def split2(x):
    high = x.astype(BF16)
    low = (x - high.astype(F32)).astype(BF16)
    return jnp.concatenate([high, low], axis=0)


def one_hot_block(lists, first, rows):
    iota = lax.broadcasted_iota(jnp.int32, (rows, lists[0].shape[1]), 0).astype(F32).astype(BF16)
    count = None
    for entry in lists:
        near = (entry - first).astype(F32).astype(BF16)
        hit = jnp.where(iota == near, jnp.ones((), BF16), jnp.zeros((), BF16))
        count = hit if count is None else count + hit
    return count


def fill_one_hot(ref, lists):
    for first in range(0, ref.shape[0], 256):
        ref[first : first + 256, :] = one_hot_block(lists, first, 256)


def local_kernel(snap_ref, conn_ref, mask_ref, vol_ref, mass_ref, hot_ref, acc_ref):
    snaps = snap_ref.shape[0]
    snap = snap_ref[...]
    snap2 = split2(snap)
    acc_ref[...] = jnp.zeros_like(acc_ref)
    for step in range(conn_ref.shape[1] // CHUNK):
        cols = slice(step * CHUNK, (step + 1) * CHUNK)
        hot = hot_ref.at[step % 2]
        fill_one_hot(hot, [conn_ref[i : i + 1, cols] for i in range(4)])
        weight = vol_ref[:, cols] * (mask_ref[:, cols].astype(F32) * 0.05)
        both = jnp.dot(snap2, hot[...], preferred_element_type=F32)
        value = (both[:snaps] + both[snaps:]) * weight
        weight2 = split2(jnp.broadcast_to(weight, (8, CHUNK)))
        left = jnp.concatenate([split2(value), weight2], axis=0)
        acc_ref[...] += lax.dot_general(left, hot[...], NT, preferred_element_type=F32)
    diag = acc_ref[2 * snaps : 2 * snaps + 1] + acc_ref[2 * snaps + 8 : 2 * snaps + 9]
    mass = acc_ref[:snaps] + acc_ref[snaps : 2 * snaps] + snap * diag
    mass_ref[...] = mass


def pick_kernel(peer_ref, back_ref, mass_ref, rows_ref, _, send_ref, slot_ref):
    mass = mass_ref[...]
    snaps = mass.shape[0]
    fill_one_hot(slot_ref, [jnp.concatenate([rows_ref[k : k + 1, :] for k in range(4)], axis=1)])
    both = jnp.dot(split2(mass), slot_ref[...], preferred_element_type=F32)
    picked = both[:snaps] + both[snaps:]
    for carrier in range(4):
        for k in range(4):
            send_ref[carrier, k] = picked[carrier * 8 : carrier * 8 + 8, k * LANES : (k + 1) * LANES]
            send_ref[carrier, 4, k : k + 1] = jnp.full((1, LANES), peer_ref[0, k], jnp.int32).astype(F32)
            send_ref[carrier, 4, 4 + k : 5 + k] = jnp.full((1, LANES), back_ref[0, k], jnp.int32).astype(F32)


def to_row(column, inside):
    return jnp.sum(jnp.where(inside, column, 0), axis=0, keepdims=True)


def spread_kernel(slots, recv_ref, send_ref, table_ref, place_ref, dma_sem):
    me = lax.axis_index("z")
    ids = jnp.concatenate([recv_ref[y, 4, 0:4] for y in range(4)], axis=0).astype(jnp.int32)
    backs = jnp.concatenate([recv_ref[y, 4, 4:8] for y in range(4)], axis=0).astype(jnp.int32)
    lane = lax.broadcasted_iota(jnp.int32, (16, LANES), 1)
    sub = lax.broadcasted_iota(jnp.int32, (16, LANES), 0)
    line = ids // 4
    key = (ids % 4) * 4 + backs
    same = (line == to_row(line, lane == sub)) & (lane < 16)
    sent = jnp.sum(jnp.where(same & (lane < sub), 1, 0), axis=1, keepdims=True)
    came = jnp.sum(jnp.where(same & (to_row(key, lane == sub) < key), 1, 0), axis=1, keepdims=True)
    home = line == me
    target = line * slots + jnp.where(home, 0, jnp.minimum(sent, slots - 1))
    source = jnp.where(
        home, zs_of(send_ref, slots) * slots + (ids % 4) * 5 + backs, line * slots + jnp.minimum(came, slots - 1)
    )
    table_ref[...] = jnp.where(lane == 0, target, source)
    copy = pltpu.make_async_copy(table_ref, place_ref, dma_sem)
    copy.start()
    send_ref[...] = jnp.zeros_like(send_ref)
    over = jnp.max(jnp.where(home, 0, sent - (slots - 1)), axis=0, keepdims=True) > 0
    copy.wait()
    for y in range(4):
        for k in range(4):
            send_ref[place_ref[y * 4 + k, 0]] = recv_ref[y, k]
    for z in range(zs_of(send_ref, slots)):
        send_ref[z * slots] = jnp.where(over, OVERFLOW, send_ref[z * slots])


def zs_of(ref, slots):
    return ref.shape[0] // slots


def collect_kernel(slots, table_ref, near_ref, far_ref, send_ref, flag_ref, place_ref, dma_sem):
    copy = pltpu.make_async_copy(table_ref, place_ref, dma_sem)
    copy.start()
    top = far_ref[0]
    for z in range(1, zs_of(far_ref, slots)):
        top = jnp.maximum(top, far_ref[z * slots])
    flag_ref[0, 0] = (jnp.max(top) > OVERFLOW * 0.5).astype(jnp.int32)
    copy.wait()
    total = far_ref.shape[0]
    for y in range(4):
        for k in range(4):
            place = place_ref[y * 4 + k, 1]
            far = far_ref[jnp.minimum(place, total - 1)]
            near = near_ref[jnp.maximum(place - total, 0)]
            send_ref[y, k] = jnp.where(place < total, far, near)


def final_kernel(recv_ref, rows_ref, live_ref, mass_ref, same_ref, other_ref, owned_ref, out_ref, gram_ref, slot_ref):
    snaps = mass_ref.shape[0]
    parts = []
    for k in range(4):
        live = live_ref[k : k + 1, :].astype(F32)
        parts.append(jnp.concatenate([recv_ref[y, k] for y in range(4)], axis=0) * live)
    fill_one_hot(slot_ref, [jnp.concatenate([rows_ref[k : k + 1, :] for k in range(4)], axis=1)])
    added = lax.dot_general(split2(jnp.concatenate(parts, axis=1)), slot_ref[...], NT, preferred_element_type=F32)
    total = mass_ref[...] + (added[:snaps] + added[snaps:])
    out_ref[...] = total
    total2 = split2(total)
    owned = owned_ref[...].astype(F32)
    core = lax.axis_index("core")
    for index, ref in ((core, same_ref), (1 - core, other_ref)):
        count = ref.shape[0]
        both = lax.dot_general(total2, split2(ref[...] * owned), NT, preferred_element_type=F32)
        gram_ref[index] = both[:snaps, :count] + (both[snaps:, :count] + both[:snaps, count:])


def gather_kernel(scale, recv_ref, out_ref):
    total = recv_ref[0]
    for z in range(1, recv_ref.shape[0]):
        total = total + recv_ref[z]
    total = total * scale
    groups, columns = total.shape[0], out_ref.shape[0]
    width = LANES // columns
    for c in range(columns):
        for half in range(groups // columns):
            out_ref[c : c + 1, half * LANES : (half + 1) * LANES] = jnp.concatenate(
                [total[half * columns + q : half * columns + q + 1, c * width : (c + 1) * width] for q in range(columns)],
                axis=1,
            )


def vmem(count):
    return [pl.BlockSpec(memory_space=pltpu.VMEM)] * count


SMEM = pl.BlockSpec(memory_space=pltpu.SMEM)
HBM = pl.BlockSpec(memory_space=pltpu.HBM)
ANY = pl.BlockSpec(memory_space=pl.ANY)


def route(recv, slots, zs):
    scratch = [pltpu.SMEM((16, LANES), jnp.int32), pltpu.SemaphoreType.DMA]
    send, table = pl.pallas_call(
        lambda *refs: spread_kernel(slots, *refs),
        out_shape=(jax.ShapeDtypeStruct((zs * slots, 8, LANES), F32), jax.ShapeDtypeStruct((16, LANES), jnp.int32)),
        in_specs=vmem(1),
        out_specs=tuple(vmem(2)),
        scratch_shapes=scratch,
        name="spread",
    )(recv)
    far = lax.all_to_all(send, "z", 0, 0, tiled=True)
    return pl.pallas_call(
        lambda *refs: collect_kernel(slots, *refs),
        out_shape=(jax.ShapeDtypeStruct((4, 4, 8, LANES), F32), jax.ShapeDtypeStruct((1, 1), jnp.int32)),
        in_specs=vmem(3),
        out_specs=(vmem(1)[0], SMEM),
        scratch_shapes=scratch,
        name="collect",
    )(table, recv.reshape(20, 8, LANES), far)


def per_device(snapshots, connect, elem_mask, volume, owned, peer_ids, peer_back, iface_rows, iface_mask):
    snaps, nodes = snapshots.shape
    zs, ys = lax.axis_size("z"), lax.axis_size("y")
    groups = lax.axis_size("x") * lax.axis_size("core")
    params = pltpu.CompilerParams(vmem_limit_bytes=40 * 1024 * 1024)
    xs, cores = lax.axis_size("x"), lax.axis_size("core")
    snaps_x = lax.all_to_all(jnp.broadcast_to(snapshots, (xs, snaps, nodes)), "x", 0, 0, tiled=True)
    snaps_x = snaps_x.reshape(xs * snaps, nodes)
    snaps_other = lax.ppermute(snaps_x, "core", [(c, (c + 1) % cores) for c in range(cores)])
    mass = pl.pallas_call(
        local_kernel,
        out_shape=jax.ShapeDtypeStruct((snaps, nodes), F32),
        in_specs=vmem(4),
        out_specs=vmem(1)[0],
        scratch_shapes=[pltpu.VMEM((2, nodes, CHUNK), BF16), pltpu.VMEM((2 * snaps + 16, nodes), F32)],
        compiler_params=params,
        cost_estimate=pl.CostEstimate(flops=10**10, bytes_accessed=10**6, transcendentals=0),
        name="local_mass",
    )(snapshots, connect, elem_mask[None], volume[None])
    send = pl.pallas_call(
        pick_kernel,
        out_shape=jax.ShapeDtypeStruct((ys, 5, 8, LANES), F32),
        in_specs=[SMEM, SMEM] + vmem(2) + [ANY],
        out_specs=vmem(1)[0],
        scratch_shapes=[pltpu.VMEM((nodes, 4 * LANES), BF16)],
        compiler_params=params,
        name="pick",
    )(peer_ids, peer_back, mass, iface_rows[0], snaps_x)
    recv = lax.all_to_all(send, "y", 0, 0, tiled=True)
    picked, short = route(recv, SLOTS, zs)
    picked = lax.cond(short[0, 0] > 0, lambda r, p: route(r, 16, zs)[0], lambda r, p: p, recv, picked)
    recv = lax.all_to_all(picked, "y", 0, 0, tiled=True)
    mass_snap, gram = pl.pallas_call(
        final_kernel,
        out_shape=(
            jax.ShapeDtypeStruct((snaps, nodes), F32),
            jax.ShapeDtypeStruct((cores, snaps, xs * snaps), F32),
        ),
        in_specs=vmem(7),
        out_specs=tuple(vmem(2)),
        scratch_shapes=[pltpu.VMEM((nodes, 4 * LANES), BF16)],
        compiler_params=params,
        name="assemble_gram",
    )(recv, iface_rows[0], iface_mask[0], mass, snaps_x, snaps_other, owned[None])
    per_z = snaps // (ys * 4)
    gram = gram.reshape(cores, per_z, ys, 4, xs, snaps).transpose(2, 4, 0, 1, 3, 5)
    gram = lax.all_to_all(gram.reshape(ys * groups, per_z * 4 * snaps), ("y", "x", "core"), 0, 0, tiled=True)
    gram = jnp.sum(gram.reshape(ys, zs, 1, 4 * snaps), axis=0)
    gram = jnp.broadcast_to(gram, (zs, groups, 4 * snaps)).reshape(zs * groups, 4 * snaps)
    gram = lax.all_to_all(gram, ("z", "x", "core"), 0, 0, tiled=True)
    gram = pl.pallas_call(
        lambda *refs: gather_kernel(1.0 / (zs * ys * nodes), *refs),
        out_shape=jax.ShapeDtypeStruct((4, groups * snaps), F32),
        in_specs=vmem(1),
        out_specs=vmem(1)[0],
        name="sum_columns",
    )(gram.reshape(zs, groups, 4 * snaps))
    return mass_snap, gram.T


def solution(mesh):
    sizes = (16, 4, 4, 2)
    fine = Mesh(mesh.devices.reshape(sizes), ("z", "y", "x", "core"))
    part, snap = ("z", "y"), ("x", "core")
    in_specs = (
        P(snap, part),
        P(None, part),
        P(part),
        P(part),
        P(part),
        P(part, None),
        P(part, None),
        P(part, None, None),
        P(part, None, None),
    )
    out_specs = (P(snap, part), P(None, part))
    return jax.shard_map(per_device, mesh=fine, in_specs=in_specs, out_specs=out_specs, check_vma=False)
```

time: 145 us -> 112 us (0.77)
  waiting for transfers between devices: 51.4 us -> 11.4 us
  between operations: 14.1 us -> 1.44 us
  blocking collectives: 40.9 us -> 51.3 us
  starting transfers between devices: 19.3 us -> 29 us
  Pallas kernels: 11.5 us -> 15.2 us
  local copies, waits for them, and re-layouts: 6.69 us -> 3.43 us
    all_gather x1 -> x0, waiting for transfers between devices: 34.8 us -> none  [per_device(): all_snaps = lax.all_gather(snapshots, ('x', 'core'), axis=0, tiled=True)]
    all_to_all x2, blocking collectives: 22.2 us -> 31.5 us  [the longest x1 22.5 us: per_device(): gram = lax.all_to_all(gram, ('z', 'x', 'core'), 0, 0, tiled=True)]
    ppermute x0 -> x1, starting transfers between devices: none -> 5.78 us  [per_device(): lax.ppermute(snaps_x, 'core', [(c, (c + 1) % cores) for c in range(cores)])]
    all_to_all x1 -> x3, waiting for transfers between devices: 15.9 us -> 11.4 us  [the longest x1 6.99 us: route(): far = lax.all_to_all(send, 'z', 0, 0, tiled=True)]
    pallas_call x1 -> x5, Pallas kernels: 9.59 us -> 13.9 us  [the longest x1 7.74 us: per_device(): pl.pallas_call(local_kernel, out_shape=jax.ShapeDtypeStruct((snaps, nodes...]
    all_to_all x1 -> x3, starting transfers between devices: 19.3 us -> 23.2 us  [the longest x1 14.9 us: route(): far = lax.all_to_all(send, 'z', 0, 0, tiled=True)]
    unnamed x18 -> x20, local copies, waits for them, and re-layouts: 5.15 us -> 1.39 us
    broadcast_in_dim x1 -> x2, local copies, waits for them, and re-layouts: 0.01 us -> 1.76 us  [the longest x1 1.75 us: per_device(): jnp.broadcast_to(snapshots, (xs, snaps, nodes))]
  transfers between devices with their start and end apart: 2 -> 4, of which waited for: 2 -> 2; matrix products, arithmetic and copies ran while one was open for 0% -> 0% of each run, Pallas kernels for 0% -> 9%
where the time goes in v2:
time: 112 us
  blocking collectives  51.3 us (46%)
  starting transfers between devices  29 us (26%)
  Pallas kernels  15.2 us (14%)
  waiting for transfers between devices  11.4 us (10%)
  local copies, waits for them, and re-layouts  3.43 us (3%)
  between operations  1.44 us (1%)
    all_to_all x1, blocking collectives, per_device(): gram = lax.all_to_all(gram, ('z', 'x', 'core'), 0, 0, tiled=True)  22.5 us
    all_to_all x1, blocking collectives, per_device(): lax.all_to_all(gram.reshape(ys * groups, per_z * 4 * snaps), ('y', 'x', '...  19.7 us
    all_to_all x1, starting transfers between devices, route(): far = lax.all_to_all(send, 'z', 0, 0, tiled=True)  14.9 us
    all_to_all x1, blocking collectives, per_device(): recv = lax.all_to_all(send, 'y', 0, 0, tiled=True)  9.04 us
    pallas_call x1, Pallas kernels, per_device(): pl.pallas_call(local_kernel, out_shape=jax.ShapeDtypeStruct((snaps, nodes...  7.74 us
    all_to_all x1, waiting for transfers between devices, route(): far = lax.all_to_all(send, 'z', 0, 0, tiled=True)  6.99 us
    ppermute x1, starting transfers between devices, per_device(): lax.ppermute(snaps_x, 'core', [(c, (c + 1) % cores) for c in range(cores)])  5.78 us
    all_to_all x1, starting transfers between devices, per_device(): lax.all_to_all(jnp.broadcast_to(snapshots, (xs, snaps, nodes)), 'x', 0, 0...  4.99 us
  transfers between devices with their start and end apart: 4, of which 2 were waited for; matrix products, arithmetic and copies ran while one was open for 0% of the time, Pallas kernels for 9%

profile of v2, /device:TPU:1, one launch (start us, length us, event | category | flops | bytes accessed | tf_op | source)
XLA Modules:
  0.0 111.8 jit_solution(16292977268473197417)
XLA Ops:
  0.6 1.7 %broadcast_in_dim.19 = f32[4,32,1024]{2,1,0:T(8,128)} broadcast(f32[32,1024]{1,0:T(8,128)} %snap_ref.1), dimensions={1,2} | broadcast | bytes 655360 | tf_op jit(solution)/shard_map/broadcast_in_dim | solution.py:195
  2.4 0.0 copy-start
  2.4 0.0 copy-start.6
  2.4 0.0 copy-start.7
  2.4 0.0 copy-start.8
  2.4 5.0 %all-to-all-start.1 = ((f32[4,32,1024]{2,1,0:T(8,128)}), f32[4,32,1024]{2,1,0:T(8,128)S(1)}, u32[]{:S(2)}, u32[]{:S(2)}) async-start(f32[4,32,1024]{2,1,0:T(8,128)} %broadcast_in_dim.19), calls=%async_computation.1 | async-start | bytes 1048576 | tf_op jit(solution)/shard_map/all_to_all | solution.py:195
  7.4 0.0 copy-done
  7.4 0.0 copy-done.6
  7.4 0.0 copy-done.7
  7.4 0.0 copy-done.8
  7.4 7.7 %local_mass.1.mass_ref = f32[32,1024]{1,0:T(8,128)S(1)} custom-call(f32[32,1024]{1,0:T(8,128)S(1)} %copy-done, s32[4,5120]{1,0:T(4,128)S(1)} %copy-done.6, s32[1,5120]{1,0:T(1,128)S(1)} %bitcast.25, f32[1,5120]{1,0:T(1,128)S(1)} %bitcast.26), custom_call_target="tpu_custom_call" | custom-call | flops 10000000000 | bytes 1000000 | tf_op jit(solution)/shard_map/local_mass/pallas_call | solution.py:198
  15.1 0.0 copy-start.1
  15.2 0.0 all-to-all-done.1
  15.2 0.0 copy-start.4
  15.2 0.0 copy-start.5
  15.2 0.6 copy-done.1
  15.8 0.0 copy-done.4
  15.8 0.0 copy-done.5
  15.8 0.8 pick.1
  16.7 9.0 %all_to_all.47.refs_0_ = f32[4,5,8,128]{3,2,1,0:T(8,128)S(1)} all-to-all(f32[4,5,8,128]{3,2,1,0:T(8,128)S(1)} %pick.1), channel_id=1, replica_groups=mesh['z'=16,'y'=4,'x'=4,'core'=2] {'y'}, dimensions={0} | all-to-all | bytes 163840 | tf_op jit(solution)/shard_map/all_to_all | solution.py:217
  25.7 1.5 %spread.3 = (f32[64,8,128]{2,1,0:T(8,128)}, s32[16,128]{1,0:T(8,128)}) custom-call(f32[4,5,8,128]{3,2,1,0:T(8,128)S(1)} %all_to_all.47.refs_0_), custom_call_target="tpu_custom_call" | custom-call | tf_op jit(solution)/shard_map/spread/pallas_call | solution.py:170
  27.2 14.9 %all-to-all-start.3 = ((f32[64,8,128]{2,1,0:T(8,128)}), f32[64,8,128]{2,1,0:T(8,128)S(1)}, u32[]{:S(2)}, u32[]{:S(2)}) async-start(f32[64,8,128]{2,1,0:T(8,128)} %get-tuple-element.17), calls=%async_computation.3 | async-start | bytes 524288 | tf_op jit(solution)/shard_map/all_to_all | solution.py:178
  42.2 5.8 %collective-permute-start = (f32[128,1024]{1,0:T(8,128)S(1)}, f32[128,1024]{1,0:T(8,128)S(1)}, u32[]{:S(2)}, u32[]{:S(2)}) collective-permute-start(f32[128,1024]{1,0:T(8,128)S(1)} %bitcast.19), channel_id=1, source_target_pairs={{0,1},{1,0},{2,3},{3,2},{4,5},{5,4},{6,7},{7,6},{8,9},{9,8},{10,11... | collective-permute-start | bytes 1572872 | tf_op jit(solution)/shard_map/ppermute | solution.py:197
  47.9 7.0 %all-to-all-done.3.refs_2_ = f32[64,8,128]{2,1,0:T(8,128)S(1)} async-done(((f32[64,8,128]{2,1,0:T(8,128)}), f32[64,8,128]{2,1,0:T(8,128)S(1)}, u32[]{:S(2)}, u32[]{:S(2)}) %all-to-all-start.3) | async-done | bytes 262176 | tf_op jit(solution)/shard_map/all_to_all | solution.py:178
  54.9 0.0 copy-start.9
  54.9 0.7 copy-done.9
  55.6 2.3 %collect.3 = (f32[4,4,8,128]{3,2,1,0:T(8,128)}, s32[1,1]{1,0:T(1,128)}) custom-call(s32[16,128]{1,0:T(8,128)} %get-tuple-element.16.refs_0_, f32[20,8,128]{2,1,0:T(8,128)S(1)} %bitcast.27, f32[64,8,128]{2,1,0:T(8,128)} %copy-done.9), custom_call_target="tpu_custom_call" | custom-call | tf_op jit(solution)/shard_map/collect/pallas_call | solution.py:179
  58.6 0.0 copy-start.2
  58.7 3.3 %all-to-all-start.4 = ((f32[4,4,8,128]{3,2,1,0:T(8,128)}), f32[4,4,8,128]{3,2,1,0:T(8,128)S(1)}, u32[]{:S(2)}, u32[]{:S(2)}) async-start(f32[4,4,8,128]{3,2,1,0:T(8,128)} %get-tuple-element.22), calls=%async_computation.4 | async-start | bytes 131072 | tf_op jit(solution)/shard_map/all_to_all | solution.py:220
  62.0 0.0 copy-start.3
  62.0 0.0 collective-permute-done.other_ref
  62.0 4.4 %all-to-all-done.4.recv_ref = f32[4,4,8,128]{3,2,1,0:T(8,128)S(1)} async-done(((f32[4,4,8,128]{3,2,1,0:T(8,128)}), f32[4,4,8,128]{3,2,1,0:T(8,128)S(1)}, u32[]{:S(2)}, u32[]{:S(2)}) %all-to-all-start.4) | async-done | bytes 65568 | tf_op jit(solution)/shard_map/all_to_all | solution.py:220
  66.4 0.0 copy-done.2
  66.4 0.0 copy-done.3
  66.4 1.2 %assemble_gram.1 = (f32[32,1024]{1,0:T(8,128)}, f32[2,32,128]{2,1,0:T(8,128)S(1)}) custom-call(f32[4,4,8,128]{3,2,1,0:T(8,128)S(1)} %all-to-all-done.4.recv_ref, s32[4,128]{1,0:T(4,128)S(1)} %bitcast.22, s32[4,128]{1,0:T(4,128)S(1)} %bitcast.24, f32[32,1024]{1,0:T(8,128)S(1)} %local_mass.1.mass_ref, f32[128,1024]{1,0:T(8,128)S(1)} %bitcast.20, ...), custom_call_target="tpu_custom_call" | custom-call | tf_op jit(solution)/shard_map/assemble_gram/pallas_call | solution.py:221
  67.7 0.1 reshape.40
  67.8 0.1 all_to_all.38
  68.0 19.7 %all_to_all.48 = f32[32,1,256]{2,1,0:T(1,128)S(1)} all-to-all(f32[32,1,256]{2,1,0:T(1,128)S(1)} %all_to_all.38), channel_id=1, replica_groups=mesh['z'=16,'y'=4,'x'=4,'core'=2] {'y','x','core'}, dimensions={0} | all-to-all | bytes 65536 | tf_op jit(solution)/shard_map/all_to_all | solution.py:235
  87.7 22.5 %all_to_all.49 = f32[128,1,128]{2,1,0:T(1,128)} all-to-all(f32[128,1,128]{2,1,0:T(1,128)S(1)} %bitcast.30), channel_id=1, replica_groups=mesh['z'=16,'y'=4,'x'=4,'core'=2] {'z','x','core'}, dimensions={0} | all-to-all | bytes 131072 | tf_op jit(solution)/shard_map/all_to_all | solution.py:238
  110.2 1.5 %sum_columns.1 = f32[4,256]{1,0:T(4,128)} custom-call(f32[16,8,128]{2,1,0:T(8,128)} %bitcast.31), custom_call_target="tpu_custom_call" | custom-call | tf_op jit(solution)/shard_map/sum_columns/pallas_call | solution.py:239
  (4 shorter events, 0.1 us)
Async XLA Ops:
  2.4 5.0 %copy-start = (f32[32,1024]{1,0:T(8,128)S(1)}, f32[32,1024]{1,0:T(8,128)}, u32[]{:S(2)}) copy-start(f32[32,1024]{1,0:T(8,128)} %snap_ref.1) | copy-start | bytes 393220
  2.4 5.0 %copy-start.6 = (s32[4,5120]{1,0:T(4,128)S(1)}, s32[4,5120]{1,0:T(4,128)}, u32[]{:S(2)}) copy-start(s32[4,5120]{1,0:T(4,128)} %conn_ref.1) | copy-start | bytes 245764
  2.4 5.0 %copy-start.7 = (s32[5120]{0:T(1024)S(1)}, s32[5120]{0:T(1024)}, u32[]{:S(2)}) copy-start(s32[5120]{0:T(1024)} %param.13) | copy-start | bytes 61444
  2.4 5.0 %copy-start.8 = (f32[5120]{0:T(1024)S(1)}, f32[5120]{0:T(1024)}, u32[]{:S(2)}) copy-start(f32[5120]{0:T(1024)} %param.14) | copy-start | bytes 61444
  2.4 12.8 %all-to-all-start.1 = ((f32[4,32,1024]{2,1,0:T(8,128)}), f32[4,32,1024]{2,1,0:T(8,128)S(1)}, u32[]{:S(2)}, u32[]{:S(2)}) async-start(f32[4,32,1024]{2,1,0:T(8,128)} %broadcast_in_dim.19), calls=%async_computation.1 | async-start | bytes 1048576 | tf_op jit(solution)/shard_map/all_to_all | solution.py:195
  15.1 0.7 copy-start.1
  15.2 0.7 copy-start.4
  15.2 0.7 copy-start.5
  27.2 27.7 %all-to-all-start.3 = ((f32[64,8,128]{2,1,0:T(8,128)}), f32[64,8,128]{2,1,0:T(8,128)S(1)}, u32[]{:S(2)}, u32[]{:S(2)}) async-start(f32[64,8,128]{2,1,0:T(8,128)} %get-tuple-element.17), calls=%async_computation.3 | async-start | bytes 524288 | tf_op jit(solution)/shard_map/all_to_all | solution.py:178
  42.2 19.8 %collective-permute-start = (f32[128,1024]{1,0:T(8,128)S(1)}, f32[128,1024]{1,0:T(8,128)S(1)}, u32[]{:S(2)}, u32[]{:S(2)}) collective-permute-start(f32[128,1024]{1,0:T(8,128)S(1)} %bitcast.19), channel_id=1, source_target_pairs={{0,1},{1,0},{2,3},{3,2},{4,5},{5,4},{6,7},{7,6},{8,9},{9,8},{10,11... | collective-permute-start | bytes 1572872 | tf_op jit(solution)/shard_map/ppermute | solution.py:197
  54.9 0.7 copy-start.9
  58.6 7.8 %copy-start.2 = (s32[1024]{0:T(1024)S(1)}, s32[1024]{0:T(1024)}, u32[]{:S(2)}) copy-start(s32[1024]{0:T(1024)} %param.15) | copy-start | bytes 12292
  58.7 7.7 %all-to-all-start.4 = ((f32[4,4,8,128]{3,2,1,0:T(8,128)}), f32[4,4,8,128]{3,2,1,0:T(8,128)S(1)}, u32[]{:S(2)}, u32[]{:S(2)}) async-start(f32[4,4,8,128]{3,2,1,0:T(8,128)} %get-tuple-element.22), calls=%async_computation.4 | async-start | bytes 131072 | tf_op jit(solution)/shard_map/all_to_all | solution.py:220
  62.0 4.4 %copy-start.3 = (s32[1,4,128]{2,1,0:T(4,128)S(1)}, s32[1,4,128]{2,1,0:T(4,128)}, u32[]{:S(2)}) copy-start(s32[1,4,128]{2,1,0:T(4,128)} %param.19) | copy-start | bytes 6148

commit v3 on v2

v3 whole, which is shorter than its diff:
```python
import jax
import jax.numpy as jnp
from jax import lax
from jax.experimental import pallas as pl
from jax.experimental.pallas import tpu as pltpu
from jax.sharding import Mesh, PartitionSpec as P

F32 = jnp.float32
BF16 = jnp.bfloat16
NT = (((1,), (1,)), ((), ()))
CHUNK = 256
LANES = 128
SLOTS = 4
OVERFLOW = 1e30


def split2(x):
    high = x.astype(BF16)
    low = (x - high.astype(F32)).astype(BF16)
    return jnp.concatenate([high, low], axis=0)


def one_hot_block(lists, first, rows):
    iota = lax.broadcasted_iota(jnp.int32, (rows, lists[0].shape[1]), 0).astype(F32).astype(BF16)
    count = None
    for entry in lists:
        near = (entry - first).astype(F32).astype(BF16)
        hit = jnp.where(iota == near, jnp.ones((), BF16), jnp.zeros((), BF16))
        count = hit if count is None else count + hit
    return count


def fill_one_hot(ref, lists):
    for first in range(0, ref.shape[0], 256):
        ref[first : first + 256, :] = one_hot_block(lists, first, 256)


def local_kernel(peer_ref, back_ref, *refs):
    far, (mass_ref, send_ref), here, (hot_ref, left_ref, acc_ref, slot_ref, sems) = refs[:6], refs[6:8], refs[8:14], refs[14:]
    copies = [pltpu.make_async_copy(a, b, sems.at[i]) for i, (a, b) in enumerate(zip(far, here))]
    for copy in copies:
        copy.start()
    snap_ref, conn_ref, mask_ref, vol_ref, rows_ref, live_ref = here
    for copy in copies:
        copy.wait()
    snaps = snap_ref.shape[0]
    snap = snap_ref[...]
    snap2 = split2(snap)
    steps = conn_ref.shape[1] // CHUNK

    def fill(step):
        cols = slice(step * CHUNK, (step + 1) * CHUNK)
        fill_one_hot(hot_ref.at[step % 2], [conn_ref[i : i + 1, cols] for i in range(4)])

    def element(step):
        cols = slice(step * CHUNK, (step + 1) * CHUNK)
        weight = vol_ref[:, cols] * (mask_ref[:, cols].astype(F32) * 0.05)
        both = jnp.dot(snap2, hot_ref[step % 2], preferred_element_type=F32)
        value = (both[:snaps] + both[snaps:]) * weight
        left_ref[step % 2] = jnp.concatenate([split2(value), split2(jnp.broadcast_to(weight, (8, CHUNK)))], axis=0)

    def add(step):
        part = lax.dot_general(left_ref[step % 2], hot_ref[step % 2], NT, preferred_element_type=F32)
        acc_ref[...] = part if step == 0 else acc_ref[...] + part

    fill(0)
    for step in range(steps):
        element(step)
        if step > 0:
            add(step - 1)
        if step + 1 < steps:
            fill(step + 1)
    add(steps - 1)
    diag = acc_ref[2 * snaps : 2 * snaps + 1] + acc_ref[2 * snaps + 8 : 2 * snaps + 9]
    mass = acc_ref[:snaps] + acc_ref[snaps : 2 * snaps] + snap * diag
    mass_ref[...] = mass
    fill_one_hot(slot_ref, [jnp.concatenate([rows_ref[k : k + 1, :] for k in range(4)], axis=1)])
    both = jnp.dot(split2(mass), slot_ref[...], preferred_element_type=F32)
    picked = both[:snaps] + both[snaps:]
    used = jnp.sum(live_ref[...].astype(F32), axis=1, keepdims=True)
    for carrier in range(4):
        for k in range(4):
            send_ref[carrier, k] = picked[carrier * 8 : carrier * 8 + 8, k * LANES : (k + 1) * LANES]
            whence = jnp.full((1, LANES), peer_ref[0, k] * 4 + back_ref[0, k], jnp.int32)
            send_ref[carrier, 4, k : k + 1] = whence.astype(F32)
        send_ref[carrier, 4, 4:8] = jnp.broadcast_to(used, (4, LANES))


def to_row(column, inside):
    return jnp.sum(jnp.where(inside, column, 0), axis=0, keepdims=True)


def spread_kernel(slots, recv_ref, send_ref, table_ref, place_ref, dma_sem):
    me = lax.axis_index("z")
    whence = jnp.concatenate([recv_ref[y, 4, 0:4] for y in range(4)], axis=0).astype(jnp.int32)
    used = jnp.concatenate([recv_ref[y, 4, 4:8] for y in range(4)], axis=0).astype(jnp.int32)
    lane = lax.broadcasted_iota(jnp.int32, (16, LANES), 1)
    sub = lax.broadcasted_iota(jnp.int32, (16, LANES), 0)
    line = whence // 16
    key = whence % 16
    same = (line == to_row(line, lane == sub)) & (lane < 16)
    width = to_row(used, lane == sub)
    sent = jnp.sum(jnp.where(same & (lane < sub), width, 0), axis=1, keepdims=True)
    came = jnp.sum(jnp.where(same & (to_row(key, lane == sub) < key), width, 0), axis=1, keepdims=True)
    home = line == me
    sent = jnp.where(home, 0, sent)
    total = send_ref.shape[0]
    last = line * slots + slots - 1
    there = line * slots + jnp.minimum(sent // LANES, slots - 1)
    here = line * slots + jnp.minimum(came // LANES, slots - 1)
    near = total + (key // 4) * 5 + key % 4
    table = jnp.where(lane == 0, there, jnp.minimum(there + 1, last))
    table = jnp.where(lane == 2, sent % LANES, table)
    table = jnp.where(lane == 3, jnp.where(home, near, here), table)
    table = jnp.where(lane == 4, jnp.where(home, near, jnp.minimum(here + 1, last)), table)
    table_ref[...] = jnp.where(lane == 5, jnp.where(home, 0, came % LANES), table)
    copy = pltpu.make_async_copy(table_ref, place_ref, dma_sem)
    copy.start()
    send_ref[...] = jnp.zeros_like(send_ref)
    over = jnp.max(jnp.where(home, 0, sent + used - slots * LANES), axis=0, keepdims=True)[:, 0:1] > 0
    tile_lane = lax.broadcasted_iota(jnp.int32, (8, LANES), 1)
    copy.wait()
    for y in range(4):
        for k in range(4):
            e = y * 4 + k
            shift = place_ref[e, 2]
            live = tile_lane < recv_ref[y, 4, 4 + k : 5 + k].astype(jnp.int32)
            moved = pltpu.roll(jnp.where(live, recv_ref[y, k], 0.0), shift, 1)
            first, second = place_ref[e, 0], place_ref[e, 1]
            send_ref[first] = send_ref[first] + jnp.where(tile_lane >= shift, moved, 0.0)
            send_ref[second] = send_ref[second] + jnp.where(tile_lane < shift, moved, 0.0)
    for z in range(zs_of(send_ref, slots)):
        send_ref[z * slots] = jnp.where(over, OVERFLOW, send_ref[z * slots])


def zs_of(ref, slots):
    return ref.shape[0] // slots


def collect_kernel(slots, table_ref, near_ref, far_ref, *refs):
    *blocks, send_ref, flag_ref, all_ref, place_ref, dma_sem = refs
    copy = pltpu.make_async_copy(table_ref, place_ref, dma_sem)
    copy.start()
    top = far_ref[0]
    for z in range(1, zs_of(far_ref, slots)):
        top = jnp.maximum(top, far_ref[z * slots])
    flag_ref[...] = jnp.where(top[0:1, 0:1] > OVERFLOW * 0.5, 1, 0)
    for index, block in enumerate(blocks):
        rows = block.shape[0]
        all_ref[index * rows : (index + 1) * rows] = block[...]
    copy.wait()
    total = far_ref.shape[0]
    tile_lane = lax.broadcasted_iota(jnp.int32, (8, LANES), 1)
    for y in range(4):
        for k in range(4):
            e = y * 4 + k
            first, second, shift = place_ref[e, 3], place_ref[e, 4], place_ref[e, 5]
            begin, rest = far_ref[jnp.minimum(first, total - 1)], far_ref[jnp.minimum(second, total - 1)]
            far = pltpu.roll(jnp.where(tile_lane >= shift, begin, rest), lax.rem(LANES - shift, LANES), 1)
            near = near_ref[jnp.maximum(first - total, 0)]
            send_ref[y, k] = jnp.where(first < total, far, near)


def final_kernel(recv_ref, rows_ref, live_ref, mass_ref, same_ref, other_ref, owned_ref, out_ref, gram_ref, slot_ref):
    snaps = mass_ref.shape[0]
    parts = []
    for k in range(4):
        live = live_ref[k : k + 1, :].astype(F32)
        parts.append(jnp.concatenate([recv_ref[y, k] for y in range(4)], axis=0) * live)
    fill_one_hot(slot_ref, [jnp.concatenate([rows_ref[k : k + 1, :] for k in range(4)], axis=1)])
    added = lax.dot_general(split2(jnp.concatenate(parts, axis=1)), slot_ref[...], NT, preferred_element_type=F32)
    total = mass_ref[...] + (added[:snaps] + added[snaps:])
    out_ref[...] = total
    total2 = split2(total)
    owned = owned_ref[...].astype(F32)
    core = lax.axis_index("core")
    here = lax.axis_index("x")
    for index, ref in ((core, same_ref), (1 - core, other_ref)):
        count = ref.shape[0]
        both = lax.dot_general(total2, split2(ref[...] * owned), NT, preferred_element_type=F32)
        terms = both[:snaps, :count] + (both[snaps:, :count] + both[:snaps, count:])
        for away in range(count // snaps):
            group = lax.rem(here + count // snaps - away, count // snaps)
            gram_ref[index, group] = terms[:, away * snaps : (away + 1) * snaps]


def gather_kernel(scale, recv_ref, out_ref):
    total = recv_ref[0]
    for z in range(1, recv_ref.shape[0]):
        total = total + recv_ref[z]
    total = total * scale
    groups, columns = total.shape[0], out_ref.shape[0]
    width = LANES // columns
    for c in range(columns):
        for half in range(groups // columns):
            out_ref[c : c + 1, half * LANES : (half + 1) * LANES] = jnp.concatenate(
                [total[half * columns + q : half * columns + q + 1, c * width : (c + 1) * width] for q in range(columns)],
                axis=1,
            )


def vmem(count):
    return [pl.BlockSpec(memory_space=pltpu.VMEM)] * count


SMEM = pl.BlockSpec(memory_space=pltpu.SMEM)
HBM = pl.BlockSpec(memory_space=pltpu.HBM)
ANY = pl.BlockSpec(memory_space=pl.ANY)


def route(recv, blocks, slots, zs):
    scratch = [pltpu.SMEM((16, LANES), jnp.int32), pltpu.SemaphoreType.DMA]
    send, table = pl.pallas_call(
        lambda *refs: spread_kernel(slots, *refs),
        out_shape=(jax.ShapeDtypeStruct((zs * slots, 8, LANES), F32), jax.ShapeDtypeStruct((16, LANES), jnp.int32)),
        in_specs=vmem(1),
        out_specs=tuple(vmem(2)),
        scratch_shapes=scratch,
        name="spread",
    )(recv)
    far = lax.all_to_all(send, "z", 0, 0, tiled=True)
    rows, nodes = blocks[0].shape
    return pl.pallas_call(
        lambda *refs: collect_kernel(slots, *refs),
        out_shape=(
            jax.ShapeDtypeStruct((4, 4, 8, LANES), F32),
            jax.ShapeDtypeStruct((1, 1), jnp.int32),
            jax.ShapeDtypeStruct((len(blocks) * rows, nodes), F32),
        ),
        in_specs=vmem(3 + len(blocks)),
        out_specs=tuple(vmem(3)),
        scratch_shapes=scratch,
        compiler_params=pltpu.CompilerParams(vmem_limit_bytes=20 * 1024 * 1024),
        name="collect",
    )(table, recv.reshape(20, 8, LANES), far, *blocks)


def per_device(snapshots, connect, elem_mask, volume, owned, peer_ids, peer_back, iface_rows, iface_mask):
    snaps, nodes = snapshots.shape
    zs, ys = lax.axis_size("z"), lax.axis_size("y")
    groups = lax.axis_size("x") * lax.axis_size("core")
    params = pltpu.CompilerParams(vmem_limit_bytes=40 * 1024 * 1024)
    xs, cores = lax.axis_size("x"), lax.axis_size("core")
    blocks = [snapshots]
    for away in range(1, xs):
        blocks.append(lax.ppermute(snapshots, "x", [(x, (x + away) % xs) for x in range(xs)]))
    given = (snapshots, connect, elem_mask[None], volume[None], iface_rows[0], iface_mask[0])
    mass, send = pl.pallas_call(
        local_kernel,
        out_shape=(jax.ShapeDtypeStruct((snaps, nodes), F32), jax.ShapeDtypeStruct((ys, 5, 8, LANES), F32)),
        in_specs=[SMEM, SMEM] + [ANY] * 6,
        out_specs=tuple(vmem(2)),
        scratch_shapes=[pltpu.VMEM(x.shape, x.dtype) for x in given]
        + [
            pltpu.VMEM((2, nodes, CHUNK), BF16),
            pltpu.VMEM((2, 2 * snaps + 16, CHUNK), BF16),
            pltpu.VMEM((2 * snaps + 16, nodes), F32),
            pltpu.VMEM((nodes, 4 * LANES), BF16),
            pltpu.SemaphoreType.DMA((6,)),
        ],
        compiler_params=pltpu.CompilerParams(vmem_limit_bytes=60 * 1024 * 1024),
        cost_estimate=pl.CostEstimate(flops=10**10, bytes_accessed=10**6, transcendentals=0),
        name="local_mass",
    )(peer_ids, peer_back, *given)
    recv = lax.all_to_all(send, "y", 0, 0, tiled=True)
    picked, short, snaps_x = route(recv, blocks, SLOTS, zs)
    snaps_other = lax.ppermute(snaps_x, "core", [(c, (c + 1) % cores) for c in range(cores)])
    picked = lax.cond(short[0, 0] > 0, lambda r, p: route(r, [r[0, 0]], 16, zs)[0], lambda r, p: p, recv, picked)
    recv = lax.all_to_all(picked, "y", 0, 0, tiled=True)
    mass_snap, gram = pl.pallas_call(
        final_kernel,
        out_shape=(
            jax.ShapeDtypeStruct((snaps, nodes), F32),
            jax.ShapeDtypeStruct((cores, xs, snaps, snaps), F32),
        ),
        in_specs=vmem(7),
        out_specs=tuple(vmem(2)),
        scratch_shapes=[pltpu.VMEM((nodes, 4 * LANES), BF16)],
        compiler_params=params,
        name="assemble_gram",
    )(recv, iface_rows[0], iface_mask[0], mass, snaps_x, snaps_other, owned[None])
    per_z = snaps // (ys * 4)
    gram = gram.reshape(cores, xs, per_z, ys, 4, snaps).transpose(3, 1, 0, 2, 4, 5)
    gram = lax.all_to_all(gram.reshape(ys * groups, per_z * 4 * snaps), ("y", "x", "core"), 0, 0, tiled=True)
    gram = jnp.sum(gram.reshape(ys, zs, 1, 4 * snaps), axis=0)
    gram = jnp.broadcast_to(gram, (zs, groups, 4 * snaps)).reshape(zs * groups, 4 * snaps)
    gram = lax.all_to_all(gram, ("z", "x", "core"), 0, 0, tiled=True)
    gram = pl.pallas_call(
        lambda *refs: gather_kernel(1.0 / (zs * ys * nodes), *refs),
        out_shape=jax.ShapeDtypeStruct((4, groups * snaps), F32),
        in_specs=vmem(1),
        out_specs=vmem(1)[0],
        name="sum_columns",
    )(gram.reshape(zs, groups, 4 * snaps))
    return mass_snap, gram.T


def solution(mesh):
    sizes = (16, 4, 4, 2)
    fine = Mesh(mesh.devices.reshape(sizes), ("z", "y", "x", "core"))
    part, snap = ("z", "y"), ("x", "core")
    in_specs = (
        P(snap, part),
        P(None, part),
        P(part),
        P(part),
        P(part),
        P(part, None),
        P(part, None),
        P(part, None, None),
        P(part, None, None),
    )
    out_specs = (P(snap, part), P(None, part))
    return jax.shard_map(per_device, mesh=fine, in_specs=in_specs, out_specs=out_specs, check_vma=False)
```

time: 112 us -> 109 us (0.973)
  waiting for transfers between devices: 11.4 us -> 3.68 us
  blocking collectives: 51.3 us -> 56.2 us
  starting transfers between devices: 29 us -> 32.9 us
  local copies, waits for them, and re-layouts: 3.43 us -> 0.21 us
    ppermute x0 -> x3, starting transfers between devices: none -> 10.5 us  [per_device(): lax.ppermute(snapshots, 'x', [(x, (x + away) % xs) for x in range(xs)])]
    all_to_all x2 -> x0, starting transfers between devices: 8.28 us -> none  [the longest x1 4.99 us: per_device(): lax.all_to_all(jnp.broadcast_to(snapshots, (xs, snaps, nodes)), 'x', 0, 0...]
    all_to_all x1, waiting for transfers between devices: 6.99 us -> 0.01 us  [route(): far = lax.all_to_all(send, 'z', 0, 0, tiled=True)]
    all_to_all x0 -> x1, blocking collectives: none -> 6.99 us  [per_device(): recv = lax.all_to_all(picked, 'y', 0, 0, tiled=True)]
    all_to_all x1, blocking collectives: 19.7 us -> 13.2 us  [per_device(): lax.all_to_all(gram.reshape(ys * groups, per_z * 4 * snaps), ('y', 'x', '...]
    all_to_all x2 -> x0, waiting for transfers between devices: 4.42 us -> none  [the longest x1 4.42 us: per_device(): recv = lax.all_to_all(picked, 'y', 0, 0, tiled=True)]
    all_to_all x1, blocking collectives: 22.5 us -> 26.3 us  [per_device(): gram = lax.all_to_all(gram, ('z', 'x', 'core'), 0, 0, tiled=True)]
    ppermute x0 -> x3, waiting for transfers between devices: none -> 3.67 us  [per_device(): lax.ppermute(snapshots, 'x', [(x, (x + away) % xs) for x in range(xs)])]
  transfers between devices with their start and end apart: 4 -> 5, of which waited for: 2 -> 2; matrix products, arithmetic and copies ran while one was open for 0% -> 0% of each run, Pallas kernels for 9% -> 0%
where the time goes in v3:
time: 109 us
  blocking collectives  56.2 us (52%)
  starting transfers between devices  32.9 us (30%)
  Pallas kernels  14.2 us (13%)
  waiting for transfers between devices  3.68 us (3%)
  between operations  1.45 us (1%)
    all_to_all x1, blocking collectives, per_device(): gram = lax.all_to_all(gram, ('z', 'x', 'core'), 0, 0, tiled=True)  26.3 us
    all_to_all x1, starting transfers between devices, route(): far = lax.all_to_all(send, 'z', 0, 0, tiled=True)  15.1 us
    all_to_all x1, blocking collectives, per_device(): lax.all_to_all(gram.reshape(ys * groups, per_z * 4 * snaps), ('y', 'x', '...  13.2 us
    ppermute x3, starting transfers between devices, per_device(): lax.ppermute(snapshots, 'x', [(x, (x + away) % xs) for x in range(xs)])  10.5 us
    all_to_all x1, blocking collectives, per_device(): recv = lax.all_to_all(send, 'y', 0, 0, tiled=True)  9.59 us
    pallas_call x1, Pallas kernels, per_device(): pl.pallas_call(local_kernel, out_shape=(jax.ShapeDtypeStruct((snaps, node...  8.46 us
    ppermute x1, starting transfers between devices, per_device(): lax.ppermute(snaps_x, 'core', [(c, (c + 1) % cores) for c in range(cores)])  7.33 us
    all_to_all x1, blocking collectives, per_device(): recv = lax.all_to_all(picked, 'y', 0, 0, tiled=True)  6.99 us
  transfers between devices with their start and end apart: 5, of which 2 were waited for; matrix products, arithmetic and copies ran while one was open for 0% of the time, Pallas kernels for 0%

profile of v3, /device:TPU:1, one launch (start us, length us, event | category | flops | bytes accessed | tf_op | source)
XLA Modules:
  0.0 108.7 jit_solution(10645013791428683162)
XLA Ops:
  0.6 8.5 %local_mass.1 = (f32[32,1024]{1,0:T(8,128)}, f32[4,5,8,128]{3,2,1,0:T(8,128)}) custom-call(s32[1,4]{1,0:T(1,128)} %peer_ref.1, s32[1,4]{1,0:T(1,128)} %back_ref.1, f32[32,1024]{1,0:T(8,128)} %refs_3_.1, s32[4,5120]{1,0:T(4,128)} %refs_1_.1, s32[1,5120]{1,0:T(1,128)} %bitcast.33, f32[1,5120]{1,0:T(1,128)} %bitcast.34, s32[4,128]{1,0:T(4,128)} %bitcast.22, ...), custom_call_target="tpu_custom_call" | custom-call | flops 10000000000 | bytes 1000000 | tf_op jit(solution)/shard_map/local_mass/pallas_call | solution.py:248
  9.1 9.6 %all_to_all.41.refs_0_ = f32[4,5,8,128]{3,2,1,0:T(8,128)S(1)} all-to-all(f32[4,5,8,128]{3,2,1,0:T(8,128)} %get-tuple-element.19), channel_id=1, replica_groups=mesh['z'=16,'y'=4,'x'=4,'core'=2] {'y'}, dimensions={0} | all-to-all | bytes 163840 | tf_op jit(solution)/shard_map/all_to_all | solution.py:265
  18.7 1.7 %spread.3 = (f32[64,8,128]{2,1,0:T(8,128)}, s32[16,128]{1,0:T(8,128)}) custom-call(f32[4,5,8,128]{3,2,1,0:T(8,128)S(1)} %all_to_all.41.refs_0_), custom_call_target="tpu_custom_call" | custom-call | tf_op jit(solution)/shard_map/spread/pallas_call | solution.py:213
  20.4 0.0 copy-start.1
  20.4 0.0 copy-start.2
  20.4 15.1 %all-to-all-start.2 = ((f32[64,8,128]{2,1,0:T(8,128)}), f32[64,8,128]{2,1,0:T(8,128)S(1)}, u32[]{:S(2)}, u32[]{:S(2)}) async-start(f32[64,8,128]{2,1,0:T(8,128)} %get-tuple-element.21), calls=%async_computation.2 | async-start | bytes 524288 | tf_op jit(solution)/shard_map/all_to_all | solution.py:221
  35.5 0.0 copy-done.1
  35.5 3.1 %collective-permute-start = (f32[32,1024]{1,0:T(8,128)S(1)}, f32[32,1024]{1,0:T(8,128)S(1)}, u32[]{:S(2)}, u32[]{:S(2)}) collective-permute-start(f32[32,1024]{1,0:T(8,128)S(1)} %copy-done.1), channel_id=1, source_target_pairs={{0,2},{2,4},{4,6},{6,0},{1,3},{3,5},{5,7},{7,1},{8,10},{10,12},{12... | collective-permute-start | bytes 393224 | tf_op jit(solution)/shard_map/ppermute | solution.py:246
  38.6 4.4 %collective-permute-start.1 = (f32[32,1024]{1,0:T(8,128)S(1)}, f32[32,1024]{1,0:T(8,128)S(1)}, u32[]{:S(2)}, u32[]{:S(2)}) collective-permute-start(f32[32,1024]{1,0:T(8,128)S(1)} %copy-done.1), channel_id=1, source_target_pairs={{0,4},{2,6},{4,0},{6,2},{1,5},{3,7},{5,1},{7,3},{8,12},{10,14},{12... | collective-permute-start | bytes 393224 | tf_op jit(solution)/shard_map/ppermute | solution.py:246
  43.0 3.1 %collective-permute-start.2 = (f32[32,1024]{1,0:T(8,128)S(1)}, f32[32,1024]{1,0:T(8,128)S(1)}, u32[]{:S(2)}, u32[]{:S(2)}) collective-permute-start(f32[32,1024]{1,0:T(8,128)S(1)} %copy-done.1), channel_id=1, source_target_pairs={{0,6},{2,0},{4,2},{6,4},{1,7},{3,1},{5,3},{7,5},{8,14},{10,8},{12,... | collective-permute-start | bytes 393224 | tf_op jit(solution)/shard_map/ppermute | solution.py:246
  46.0 0.0 collective-permute-done.refs_4_
  46.1 1.1 %collective-permute-done.1.refs_5_ = f32[32,1024]{1,0:T(8,128)S(1)} collective-permute-done((f32[32,1024]{1,0:T(8,128)S(1)}, f32[32,1024]{1,0:T(8,128)S(1)}, u32[]{:S(2)}, u32[]{:S(2)}) %collective-permute-start.1) | collective-permute-done | bytes 131104 | tf_op jit(solution)/shard_map/ppermute | solution.py:246
  47.2 2.5 %collective-permute-done.2.refs_6_ = f32[32,1024]{1,0:T(8,128)S(1)} collective-permute-done((f32[32,1024]{1,0:T(8,128)S(1)}, f32[32,1024]{1,0:T(8,128)S(1)}, u32[]{:S(2)}, u32[]{:S(2)}) %collective-permute-start.2) | collective-permute-done | bytes 131104 | tf_op jit(solution)/shard_map/ppermute | solution.py:246
  49.7 0.0 all-to-all-done.2.refs_2_
  49.7 0.0 copy-done.2
  49.7 1.3 %collect.3 = (f32[4,4,8,128]{3,2,1,0:T(8,128)S(1)}, s32[1,1]{1,0:T(1,128)}, f32[128,1024]{1,0:T(8,128)S(1)}) custom-call(s32[16,128]{1,0:T(8,128)S(1)} %copy-done.2, f32[20,8,128]{2,1,0:T(8,128)S(1)} %bitcast.26, f32[64,8,128]{2,1,0:T(8,128)S(1)} %all-to-all-done.2.refs_2_, f32[32,1024]{1,0:T(8,128)S(1)} %copy-done.1, ...), custom_call_target="tpu_custom_call" | custom-call | tf_op jit(solution)/shard_map/collect/pallas_call | solution.py:223
  51.0 7.3 %collective-permute-start.3 = (f32[128,1024]{1,0:T(8,128)S(1)}, f32[128,1024]{1,0:T(8,128)S(1)}, u32[]{:S(2)}, u32[]{:S(2)}) collective-permute-start(f32[128,1024]{1,0:T(8,128)S(1)} %get-tuple-element.25.same_ref), channel_id=1, source_target_pairs={{0,1},{1,0},{2,3},{3,2},{4,5},{5,4},{6,7},{7,6},{8,9},{9,8},{10,11... | collective-permute-start | bytes 1572872 | tf_op jit(solution)/shard_map/ppermute | solution.py:267
  59.0 0.0 copy-start.5
  59.0 0.0 copy-start.6
  59.1 0.0 copy-start
  59.1 0.0 copy-start.4
  59.1 7.0 %all_to_all.42.recv_ref = f32[4,4,8,128]{3,2,1,0:T(8,128)S(1)} all-to-all(f32[4,4,8,128]{3,2,1,0:T(8,128)S(1)} %get-tuple-element.28), channel_id=1, replica_groups=mesh['z'=16,'y'=4,'x'=4,'core'=2] {'y'}, dimensions={0} | all-to-all | bytes 131072 | tf_op jit(solution)/shard_map/all_to_all | solution.py:269
  66.1 0.0 collective-permute-done.3.other_ref
  66.1 0.0 copy-done.5
  66.1 0.0 copy-done.6
  66.1 0.0 copy-done
  66.1 0.0 copy-done.4
  66.1 1.3 %assemble_gram.1 = (f32[32,1024]{1,0:T(8,128)}, f32[2,4,32,32]{3,2,1,0:T(8,128)S(1)}) custom-call(f32[4,4,8,128]{3,2,1,0:T(8,128)S(1)} %all_to_all.42.recv_ref, s32[4,128]{1,0:T(4,128)S(1)} %bitcast.23, s32[4,128]{1,0:T(4,128)S(1)} %bitcast.25, f32[32,1024]{1,0:T(8,128)S(1)} %copy-done, f32[128,1024]{1,0:T(8,128)S(1)} %get-tuple-element.25.same_ref, ...), custom_call_target="tpu_custom_call" | custom-call | tf_op jit(solution)/shard_map/assemble_gram/pallas_call | solution.py:270
  67.4 0.1 all_to_all.34
  67.5 13.2 %all_to_all.43 = f32[32,1,256]{2,1,0:T(1,128)S(1)} all-to-all(f32[32,1,256]{2,1,0:T(1,128)S(1)} %all_to_all.34), channel_id=1, replica_groups=mesh['z'=16,'y'=4,'x'=4,'core'=2] {'y','x','core'}, dimensions={0} | all-to-all | bytes 65536 | tf_op jit(solution)/shard_map/all_to_all | solution.py:284
  80.8 26.3 %all_to_all.44 = f32[128,1,128]{2,1,0:T(1,128)} all-to-all(f32[128,1,128]{2,1,0:T(1,128)S(1)} %bitcast.29), channel_id=1, replica_groups=mesh['z'=16,'y'=4,'x'=4,'core'=2] {'z','x','core'}, dimensions={0} | all-to-all | bytes 131072 | tf_op jit(solution)/shard_map/all_to_all | solution.py:287
  107.1 1.5 %sum_columns.1 = f32[4,256]{1,0:T(4,128)} custom-call(f32[16,8,128]{2,1,0:T(8,128)} %bitcast.30), custom_call_target="tpu_custom_call" | custom-call | tf_op jit(solution)/shard_map/sum_columns/pallas_call | solution.py:288
  (4 shorter events, 0.0 us)
Async XLA Ops:
  20.4 15.1 %copy-start.1 = (f32[32,1024]{1,0:T(8,128)S(1)}, f32[32,1024]{1,0:T(8,128)}, u32[]{:S(2)}) copy-start(f32[32,1024]{1,0:T(8,128)} %refs_3_.1) | copy-start | bytes 393220
  20.4 29.3 %copy-start.2 = (s32[16,128]{1,0:T(8,128)S(1)}, s32[16,128]{1,0:T(8,128)}, u32[]{:S(2)}) copy-start(s32[16,128]{1,0:T(8,128)} %get-tuple-element.20.refs_0_) | copy-start | bytes 24580
  20.4 29.3 %all-to-all-start.2 = ((f32[64,8,128]{2,1,0:T(8,128)}), f32[64,8,128]{2,1,0:T(8,128)S(1)}, u32[]{:S(2)}, u32[]{:S(2)}) async-start(f32[64,8,128]{2,1,0:T(8,128)} %get-tuple-element.21), calls=%async_computation.2 | async-start | bytes 524288 | tf_op jit(solution)/shard_map/all_to_all | solution.py:221
  35.5 10.6 %collective-permute-start = (f32[32,1024]{1,0:T(8,128)S(1)}, f32[32,1024]{1,0:T(8,128)S(1)}, u32[]{:S(2)}, u32[]{:S(2)}) collective-permute-start(f32[32,1024]{1,0:T(8,128)S(1)} %copy-done.1), channel_id=1, source_target_pairs={{0,2},{2,4},{4,6},{6,0},{1,3},{3,5},{5,7},{7,1},{8,10},{10,12},{12... | collective-permute-start | bytes 393224 | tf_op jit(solution)/shard_map/ppermute | solution.py:246
  38.6 8.6 %collective-permute-start.1 = (f32[32,1024]{1,0:T(8,128)S(1)}, f32[32,1024]{1,0:T(8,128)S(1)}, u32[]{:S(2)}, u32[]{:S(2)}) collective-permute-start(f32[32,1024]{1,0:T(8,128)S(1)} %copy-done.1), channel_id=1, source_target_pairs={{0,4},{2,6},{4,0},{6,2},{1,5},{3,7},{5,1},{7,3},{8,12},{10,14},{12... | collective-permute-start | bytes 393224 | tf_op jit(solution)/shard_map/ppermute | solution.py:246
  43.0 6.7 %collective-permute-start.2 = (f32[32,1024]{1,0:T(8,128)S(1)}, f32[32,1024]{1,0:T(8,128)S(1)}, u32[]{:S(2)}, u32[]{:S(2)}) collective-permute-start(f32[32,1024]{1,0:T(8,128)S(1)} %copy-done.1), channel_id=1, source_target_pairs={{0,6},{2,0},{4,2},{6,4},{1,7},{3,1},{5,3},{7,5},{8,14},{10,8},{12,... | collective-permute-start | bytes 393224 | tf_op jit(solution)/shard_map/ppermute | solution.py:246
  51.0 15.0 %collective-permute-start.3 = (f32[128,1024]{1,0:T(8,128)S(1)}, f32[128,1024]{1,0:T(8,128)S(1)}, u32[]{:S(2)}, u32[]{:S(2)}) collective-permute-start(f32[128,1024]{1,0:T(8,128)S(1)} %get-tuple-element.25.same_ref), channel_id=1, source_target_pairs={{0,1},{1,0},{2,3},{3,2},{4,5},{5,4},{6,7},{7,6},{8,9},{9,8},{10,11... | collective-permute-start | bytes 1572872 | tf_op jit(solution)/shard_map/ppermute | solution.py:267
  59.0 7.1 %copy-start.5 = (s32[1,4,128]{2,1,0:T(4,128)S(1)}, s32[1,4,128]{2,1,0:T(4,128)}, u32[]{:S(2)}) copy-start(s32[1,4,128]{2,1,0:T(4,128)} %param.18) | copy-start | bytes 6148
  59.0 7.0 %copy-start.6 = (s32[1,4,128]{2,1,0:T(4,128)S(1)}, s32[1,4,128]{2,1,0:T(4,128)}, u32[]{:S(2)}) copy-start(s32[1,4,128]{2,1,0:T(4,128)} %param.19) | copy-start | bytes 6148
  59.1 7.0 %copy-start = (f32[32,1024]{1,0:T(8,128)S(1)}, f32[32,1024]{1,0:T(8,128)}, u32[]{:S(2)}) copy-start(f32[32,1024]{1,0:T(8,128)} %get-tuple-element.24.mass_ref) | copy-start | bytes 393220
  59.1 7.0 %copy-start.4 = (s32[1024]{0:T(1024)S(1)}, s32[1024]{0:T(1024)}, u32[]{:S(2)}) copy-start(s32[1024]{0:T(1024)} %param.15) | copy-start | bytes 12292

commit v4 on v3

--- a/solution.py
+++ b/solution.py
@@ -35,46 +35,55 @@
         ref[first : first + 256, :] = one_hot_block(lists, first, 256)
 
 
-def local_kernel(peer_ref, back_ref, *refs):
-    far, (mass_ref, send_ref), here, (hot_ref, left_ref, acc_ref, slot_ref, sems) = refs[:6], refs[6:8], refs[8:14], refs[14:]
+def local_kernel(*refs):
+    far, (out_ref, send_ref), here = refs[:8], refs[8:10], refs[10:18]
+    hot_ref, turned_ref, left_ref, acc_ref, slot_ref, mass_ref, sems = refs[18:]
     copies = [pltpu.make_async_copy(a, b, sems.at[i]) for i, (a, b) in enumerate(zip(far, here))]
     for copy in copies:
         copy.start()
-    snap_ref, conn_ref, mask_ref, vol_ref, rows_ref, live_ref = here
-    for copy in copies:
-        copy.wait()
+    conn_ref, mask_ref, vol_ref, snap_ref, rows_ref, live_ref, peer_ref, back_ref = here
     snaps = snap_ref.shape[0]
-    snap = snap_ref[...]
-    snap2 = split2(snap)
     steps = conn_ref.shape[1] // CHUNK
 
     def fill(step):
         cols = slice(step * CHUNK, (step + 1) * CHUNK)
-        fill_one_hot(hot_ref.at[step % 2], [conn_ref[i : i + 1, cols] for i in range(4)])
+        lists = [conn_ref[i : i + 1, cols] for i in range(4)]
+        for first in range(0, hot_ref.shape[1], 256):
+            block = one_hot_block(lists, first, 256)
+            hot_ref[step % 3, first : first + 256, :] = block
+            turned_ref[step % 3, :, first : first + 256] = block.T
 
     def element(step):
         cols = slice(step * CHUNK, (step + 1) * CHUNK)
         weight = vol_ref[:, cols] * (mask_ref[:, cols].astype(F32) * 0.05)
-        both = jnp.dot(snap2, hot_ref[step % 2], preferred_element_type=F32)
+        both = jnp.dot(snap2, hot_ref[step % 3], preferred_element_type=F32)
         value = (both[:snaps] + both[snaps:]) * weight
-        left_ref[step % 2] = jnp.concatenate([split2(value), split2(jnp.broadcast_to(weight, (8, CHUNK)))], axis=0)
+        left_ref[step % 3] = jnp.concatenate([split2(value), split2(jnp.broadcast_to(weight, (8, CHUNK)))], axis=0)
 
     def add(step):
-        part = lax.dot_general(left_ref[step % 2], hot_ref[step % 2], NT, preferred_element_type=F32)
+        part = jnp.dot(left_ref[step % 3], turned_ref[step % 3], preferred_element_type=F32)
         acc_ref[...] = part if step == 0 else acc_ref[...] + part
 
+    copies[0].wait()
     fill(0)
+    for copy in copies[1:]:
+        copy.wait()
+    snap = snap_ref[...]
+    snap2 = split2(snap)
+    fill_one_hot(slot_ref, [jnp.concatenate([rows_ref[k : k + 1, :] for k in range(4)], axis=1)])
+    fill(1)
     for step in range(steps):
         element(step)
         if step > 0:
             add(step - 1)
-        if step + 1 < steps:
-            fill(step + 1)
+        if step + 2 < steps:
+            fill(step + 2)
     add(steps - 1)
     diag = acc_ref[2 * snaps : 2 * snaps + 1] + acc_ref[2 * snaps + 8 : 2 * snaps + 9]
     mass = acc_ref[:snaps] + acc_ref[snaps : 2 * snaps] + snap * diag
     mass_ref[...] = mass
-    fill_one_hot(slot_ref, [jnp.concatenate([rows_ref[k : k + 1, :] for k in range(4)], axis=1)])
+    copy = pltpu.make_async_copy(mass_ref, out_ref, sems.at[8])
+    copy.start()
     both = jnp.dot(split2(mass), slot_ref[...], preferred_element_type=F32)
     picked = both[:snaps] + both[snaps:]
     used = jnp.sum(live_ref[...].astype(F32), axis=1, keepdims=True)
@@ -84,13 +93,22 @@
             whence = jnp.full((1, LANES), peer_ref[0, k] * 4 + back_ref[0, k], jnp.int32)
             send_ref[carrier, 4, k : k + 1] = whence.astype(F32)
         send_ref[carrier, 4, 4:8] = jnp.broadcast_to(used, (4, LANES))
+    copy.wait()
 
 
 def to_row(column, inside):
     return jnp.sum(jnp.where(inside, column, 0), axis=0, keepdims=True)
 
 
-def spread_kernel(slots, recv_ref, send_ref, table_ref, place_ref, dma_sem):
+def pack(first, second, shift):
+    return second * (1 << 19) + first * (1 << 7) + shift
+
+
+def unpack(word):
+    return (word >> 7) & 4095, word >> 19, word & 127
+
+
+def spread_kernel(slots, recv_ref, send_ref, table_ref):
     me = lax.axis_index("z")
     whence = jnp.concatenate([recv_ref[y, 4, 0:4] for y in range(4)], axis=0).astype(jnp.int32)
     used = jnp.concatenate([recv_ref[y, 4, 4:8] for y in range(4)], axis=0).astype(jnp.int32)
@@ -109,24 +127,19 @@
     there = line * slots + jnp.minimum(sent // LANES, slots - 1)
     here = line * slots + jnp.minimum(came // LANES, slots - 1)
     near = total + (key // 4) * 5 + key % 4
-    table = jnp.where(lane == 0, there, jnp.minimum(there + 1, last))
-    table = jnp.where(lane == 2, sent % LANES, table)
-    table = jnp.where(lane == 3, jnp.where(home, near, here), table)
-    table = jnp.where(lane == 4, jnp.where(home, near, jnp.minimum(here + 1, last)), table)
-    table_ref[...] = jnp.where(lane == 5, jnp.where(home, 0, came % LANES), table)
-    copy = pltpu.make_async_copy(table_ref, place_ref, dma_sem)
-    copy.start()
+    table_ref[...] = jnp.broadcast_to(
+        jnp.where(home, near * ((1 << 19) + (1 << 7)), pack(here, jnp.minimum(here + 1, last), came % LANES)), (16, LANES)
+    )
+    word = pack(there, jnp.minimum(there + 1, last), sent % LANES)
     send_ref[...] = jnp.zeros_like(send_ref)
     over = jnp.max(jnp.where(home, 0, sent + used - slots * LANES), axis=0, keepdims=True)[:, 0:1] > 0
     tile_lane = lax.broadcasted_iota(jnp.int32, (8, LANES), 1)
-    copy.wait()
     for y in range(4):
         for k in range(4):
             e = y * 4 + k
-            shift = place_ref[e, 2]
+            first, second, shift = unpack(word[e, 0])
             live = tile_lane < recv_ref[y, 4, 4 + k : 5 + k].astype(jnp.int32)
             moved = pltpu.roll(jnp.where(live, recv_ref[y, k], 0.0), shift, 1)
-            first, second = place_ref[e, 0], place_ref[e, 1]
             send_ref[first] = send_ref[first] + jnp.where(tile_lane >= shift, moved, 0.0)
             send_ref[second] = send_ref[second] + jnp.where(tile_lane < shift, moved, 0.0)
     for z in range(zs_of(send_ref, slots)):
@@ -137,24 +150,25 @@
     return ref.shape[0] // slots
 
 
-def collect_kernel(slots, table_ref, near_ref, far_ref, *refs):
-    *blocks, send_ref, flag_ref, all_ref, place_ref, dma_sem = refs
-    copy = pltpu.make_async_copy(table_ref, place_ref, dma_sem)
-    copy.start()
+def collect_kernel(slots, table_ref, near_ref, far_ref, owned_ref, rows_ref, live_ref, *refs):
+    *blocks, send_ref, flag_ref, all_ref, count_ref, list_ref, used_ref = refs
+    table = table_ref[...]
     top = far_ref[0]
     for z in range(1, zs_of(far_ref, slots)):
         top = jnp.maximum(top, far_ref[z * slots])
     flag_ref[...] = jnp.where(top[0:1, 0:1] > OVERFLOW * 0.5, 1, 0)
+    count_ref[...] = owned_ref[...].astype(F32)
+    list_ref[...] = rows_ref[...]
+    used_ref[...] = live_ref[...].astype(F32)
     for index, block in enumerate(blocks):
         rows = block.shape[0]
         all_ref[index * rows : (index + 1) * rows] = block[...]
-    copy.wait()
     total = far_ref.shape[0]
     tile_lane = lax.broadcasted_iota(jnp.int32, (8, LANES), 1)
     for y in range(4):
         for k in range(4):
             e = y * 4 + k
-            first, second, shift = place_ref[e, 3], place_ref[e, 4], place_ref[e, 5]
+            first, second, shift = unpack(table[e, 0])
             begin, rest = far_ref[jnp.minimum(first, total - 1)], far_ref[jnp.minimum(second, total - 1)]
             far = pltpu.roll(jnp.where(tile_lane >= shift, begin, rest), lax.rem(LANES - shift, LANES), 1)
             near = near_ref[jnp.maximum(first - total, 0)]
@@ -165,14 +179,14 @@
     snaps = mass_ref.shape[0]
     parts = []
     for k in range(4):
-        live = live_ref[k : k + 1, :].astype(F32)
+        live = live_ref[k : k + 1, :]
         parts.append(jnp.concatenate([recv_ref[y, k] for y in range(4)], axis=0) * live)
     fill_one_hot(slot_ref, [jnp.concatenate([rows_ref[k : k + 1, :] for k in range(4)], axis=1)])
     added = lax.dot_general(split2(jnp.concatenate(parts, axis=1)), slot_ref[...], NT, preferred_element_type=F32)
     total = mass_ref[...] + (added[:snaps] + added[snaps:])
     out_ref[...] = total
     total2 = split2(total)
-    owned = owned_ref[...].astype(F32)
+    owned = owned_ref[...]
     core = lax.axis_index("core")
     here = lax.axis_index("x")
     for index, ref in ((core, same_ref), (1 - core, other_ref)):
@@ -191,31 +205,36 @@
     total = total * scale
     groups, columns = total.shape[0], out_ref.shape[0]
     width = LANES // columns
-    for c in range(columns):
-        for half in range(groups // columns):
-            out_ref[c : c + 1, half * LANES : (half + 1) * LANES] = jnp.concatenate(
-                [total[half * columns + q : half * columns + q + 1, c * width : (c + 1) * width] for q in range(columns)],
-                axis=1,
-            )
+    block = lax.broadcasted_iota(jnp.int32, (groups, LANES), 1) // width
+    place = lax.broadcasted_iota(jnp.int32, (groups, LANES), 0) % columns
+    out = jnp.zeros((groups, LANES), F32)
+    for away in range(columns):
+        turned = total if away == 0 else pltpu.roll(total, away * width, 1)
+        turned = jnp.where(block == place, turned, 0.0)
+        if away > 0:
+            near = pltpu.roll(turned, groups - away, 0)
+            wrapped = pltpu.roll(turned, (groups - away + columns) % groups, 0)
+            turned = jnp.where(place + away < columns, near, wrapped)
+        out = out + turned
+    for half in range(groups // columns):
+        out_ref[:, half * LANES : (half + 1) * LANES] = out[half * columns : (half + 1) * columns]
 
 
 def vmem(count):
     return [pl.BlockSpec(memory_space=pltpu.VMEM)] * count
 
 
-SMEM = pl.BlockSpec(memory_space=pltpu.SMEM)
-HBM = pl.BlockSpec(memory_space=pltpu.HBM)
 ANY = pl.BlockSpec(memory_space=pl.ANY)
-
-
-def route(recv, blocks, slots, zs):
-    scratch = [pltpu.SMEM((16, LANES), jnp.int32), pltpu.SemaphoreType.DMA]
+SMALL = pltpu.CompilerParams(vmem_limit_bytes=20 * 1024 * 1024)
+
+
+def route(recv, blocks, owned, lists, live, slots, zs):
     send, table = pl.pallas_call(
         lambda *refs: spread_kernel(slots, *refs),
         out_shape=(jax.ShapeDtypeStruct((zs * slots, 8, LANES), F32), jax.ShapeDtypeStruct((16, LANES), jnp.int32)),
         in_specs=vmem(1),
         out_specs=tuple(vmem(2)),
-        scratch_shapes=scratch,
+        compiler_params=SMALL,
         name="spread",
     )(recv)
     far = lax.all_to_all(send, "z", 0, 0, tiled=True)
@@ -226,13 +245,15 @@
             jax.ShapeDtypeStruct((4, 4, 8, LANES), F32),
             jax.ShapeDtypeStruct((1, 1), jnp.int32),
             jax.ShapeDtypeStruct((len(blocks) * rows, nodes), F32),
+            jax.ShapeDtypeStruct(owned.shape, F32),
+            jax.ShapeDtypeStruct(lists.shape, jnp.int32),
+            jax.ShapeDtypeStruct(live.shape, F32),
         ),
-        in_specs=vmem(3 + len(blocks)),
-        out_specs=tuple(vmem(3)),
-        scratch_shapes=scratch,
-        compiler_params=pltpu.CompilerParams(vmem_limit_bytes=20 * 1024 * 1024),
+        in_specs=vmem(6 + len(blocks)),
+        out_specs=tuple(vmem(6)),
+        compiler_params=SMALL,
         name="collect",
-    )(table, recv.reshape(20, 8, LANES), far, *blocks)
+    )(table, recv.reshape(20, 8, LANES), far, owned, lists, live, *blocks)
 
 
 def per_device(snapshots, connect, elem_mask, volume, owned, peer_ids, peer_back, iface_rows, iface_mask):
@@ -244,28 +265,34 @@
     blocks = [snapshots]
     for away in range(1, xs):
         blocks.append(lax.ppermute(snapshots, "x", [(x, (x + away) % xs) for x in range(xs)]))
-    given = (snapshots, connect, elem_mask[None], volume[None], iface_rows[0], iface_mask[0])
+    given = (connect, elem_mask[None], volume[None], snapshots, iface_rows[0], iface_mask[0])
+    room = [pltpu.VMEM(x.shape, x.dtype) for x in given] + [pltpu.SMEM(peer_ids.shape, jnp.int32)] * 2
     mass, send = pl.pallas_call(
         local_kernel,
         out_shape=(jax.ShapeDtypeStruct((snaps, nodes), F32), jax.ShapeDtypeStruct((ys, 5, 8, LANES), F32)),
-        in_specs=[SMEM, SMEM] + [ANY] * 6,
-        out_specs=tuple(vmem(2)),
-        scratch_shapes=[pltpu.VMEM(x.shape, x.dtype) for x in given]
+        in_specs=[ANY] * 8,
+        out_specs=(ANY, vmem(1)[0]),
+        scratch_shapes=room
         + [
-            pltpu.VMEM((2, nodes, CHUNK), BF16),
-            pltpu.VMEM((2, 2 * snaps + 16, CHUNK), BF16),
+            pltpu.VMEM((3, nodes, CHUNK), BF16),
+            pltpu.VMEM((3, CHUNK, nodes), BF16),
+            pltpu.VMEM((3, 2 * snaps + 16, CHUNK), BF16),
             pltpu.VMEM((2 * snaps + 16, nodes), F32),
             pltpu.VMEM((nodes, 4 * LANES), BF16),
-            pltpu.SemaphoreType.DMA((6,)),
+            pltpu.VMEM((snaps, nodes), F32),
+            pltpu.SemaphoreType.DMA((9,)),
         ],
         compiler_params=pltpu.CompilerParams(vmem_limit_bytes=60 * 1024 * 1024),
         cost_estimate=pl.CostEstimate(flops=10**10, bytes_accessed=10**6, transcendentals=0),
         name="local_mass",
-    )(peer_ids, peer_back, *given)
+    )(*given, peer_ids, peer_back)
     recv = lax.all_to_all(send, "y", 0, 0, tiled=True)
-    picked, short, snaps_x = route(recv, blocks, SLOTS, zs)
+    picked, short, snaps_x, counted, lists, live = route(
+        recv, blocks, owned[None], iface_rows[0], iface_mask[0], SLOTS, zs
+    )
+    none = jnp.zeros((4, LANES), jnp.int32)
     snaps_other = lax.ppermute(snaps_x, "core", [(c, (c + 1) % cores) for c in range(cores)])
-    picked = lax.cond(short[0, 0] > 0, lambda r, p: route(r, [r[0, 0]], 16, zs)[0], lambda r, p: p, recv, picked)
+    picked = lax.cond(short[0, 0] > 0, lambda r, p: route(r, [r[0, 0]], none, none, none, 16, zs)[0], lambda r, p: p, recv, picked)
     recv = lax.all_to_all(picked, "y", 0, 0, tiled=True)
     mass_snap, gram = pl.pallas_call(
         final_kernel,
@@ -278,7 +305,7 @@
         scratch_shapes=[pltpu.VMEM((nodes, 4 * LANES), BF16)],
         compiler_params=params,
         name="assemble_gram",
-    )(recv, iface_rows[0], iface_mask[0], mass, snaps_x, snaps_other, owned[None])
+    )(recv, lists, live, mass, snaps_x, snaps_other, counted)
     per_z = snaps // (ys * 4)
     gram = gram.reshape(cores, xs, per_z, ys, 4, snaps).transpose(3, 1, 0, 2, 4, 5)
     gram = lax.all_to_all(gram.reshape(ys * groups, per_z * 4 * snaps), ("y", "x", "core"), 0, 0, tiled=True)
@@ -290,6 +317,7 @@
         out_shape=jax.ShapeDtypeStruct((4, groups * snaps), F32),
         in_specs=vmem(1),
         out_specs=vmem(1)[0],
+        compiler_params=SMALL,
         name="sum_columns",
     )(gram.reshape(zs, groups, 4 * snaps))
     return mass_snap, gram.T

time: 109 us -> 106 us (0.972)
  Pallas kernels: 14.2 us -> 11.4 us
where the time goes in v4:
time: 106 us
  blocking collectives  56.1 us (53%)
  starting transfers between devices  32.9 us (31%)
  Pallas kernels  11.4 us (11%)
  waiting for transfers between devices  3.68 us (3%)
  between operations  1.4 us (1%)
    all_to_all x1, blocking collectives, per_device(): gram = lax.all_to_all(gram, ('z', 'x', 'core'), 0, 0, tiled=True)  26.3 us
    all_to_all x1, starting transfers between devices, route(): far = lax.all_to_all(send, 'z', 0, 0, tiled=True)  15 us
    all_to_all x1, blocking collectives, per_device(): lax.all_to_all(gram.reshape(ys * groups, per_z * 4 * snaps), ('y', 'x', '...  13.2 us
    ppermute x3, starting transfers between devices, per_device(): lax.ppermute(snapshots, 'x', [(x, (x + away) % xs) for x in range(xs)])  10.5 us
    all_to_all x1, blocking collectives, per_device(): recv = lax.all_to_all(send, 'y', 0, 0, tiled=True)  9.59 us
    pallas_call x1, Pallas kernels, per_device(): pl.pallas_call(local_kernel, out_shape=(jax.ShapeDtypeStruct((snaps, node...  7.59 us
    ppermute x1, starting transfers between devices, per_device(): lax.ppermute(snaps_x, 'core', [(c, (c + 1) % cores) for c in range(cores)])  7.3 us
    all_to_all x1, blocking collectives, per_device(): recv = lax.all_to_all(picked, 'y', 0, 0, tiled=True)  6.99 us
  transfers between devices with their start and end apart: 5, of which 2 were waited for; matrix products, arithmetic and copies ran while one was open for 0% of the time, Pallas kernels for 0%

profile of v4, /device:TPU:1, one launch (start us, length us, event | category | flops | bytes accessed | tf_op | source)
XLA Modules:
  0.0 105.6 jit_solution(3196992956312305142)
XLA Ops:
  0.6 7.6 %local_mass.1 = (f32[32,1024]{1,0:T(8,128)}, f32[4,5,8,128]{3,2,1,0:T(8,128)}) custom-call(s32[4,5120]{1,0:T(4,128)} %refs_0_.2, s32[1,5120]{1,0:T(1,128)} %bitcast.33, f32[1,5120]{1,0:T(1,128)} %bitcast.34, f32[32,1024]{1,0:T(8,128)} %refs_6_.3, s32[4,128]{1,0:T(4,128)} %bitcast.23, s32[4,128]{1,0:T(4,128)} %bitcast.25, s32[1,4]{1,0:T(1,128)} %refs_6_.2, ...), custom_call_target="tpu_custom_call" | custom-call | flops 10000000000 | bytes 1000000 | tf_op jit(solution)/shard_map/local_mass/pallas_call | solution.py:270
  8.2 9.6 %all_to_all.41.refs_0_ = f32[4,5,8,128]{3,2,1,0:T(8,128)S(1)} all-to-all(f32[4,5,8,128]{3,2,1,0:T(8,128)} %get-tuple-element.22), channel_id=1, replica_groups=mesh['z'=16,'y'=4,'x'=4,'core'=2] {'y'}, dimensions={0} | all-to-all | bytes 163840 | tf_op jit(solution)/shard_map/all_to_all | solution.py:289
  17.8 1.1 %spread.3 = (f32[64,8,128]{2,1,0:T(8,128)}, s32[16,128]{1,0:T(8,128)S(1)}) custom-call(f32[4,5,8,128]{3,2,1,0:T(8,128)S(1)} %all_to_all.41.refs_0_), custom_call_target="tpu_custom_call" | custom-call | tf_op jit(solution)/shard_map/spread/pallas_call | solution.py:232
  19.0 0.0 copy-start
  19.0 0.0 copy-start.3
  19.0 0.0 copy-start.4
  19.0 15.0 %all-to-all-start.2 = ((f32[64,8,128]{2,1,0:T(8,128)}), f32[64,8,128]{2,1,0:T(8,128)S(1)}, u32[]{:S(2)}, u32[]{:S(2)}) async-start(f32[64,8,128]{2,1,0:T(8,128)} %get-tuple-element.24), calls=%async_computation.2 | async-start | bytes 524288 | tf_op jit(solution)/shard_map/all_to_all | solution.py:240
  34.0 0.0 copy-done
  34.0 0.0 copy-start.2
  34.0 3.1 %collective-permute-start = (f32[32,1024]{1,0:T(8,128)S(1)}, f32[32,1024]{1,0:T(8,128)S(1)}, u32[]{:S(2)}, u32[]{:S(2)}) collective-permute-start(f32[32,1024]{1,0:T(8,128)S(1)} %copy-done), channel_id=1, source_target_pairs={{0,2},{2,4},{4,6},{6,0},{1,3},{3,5},{5,7},{7,1},{8,10},{10,12},{12... | collective-permute-start | bytes 393224 | tf_op jit(solution)/shard_map/ppermute | solution.py:267
  37.2 4.4 %collective-permute-start.1 = (f32[32,1024]{1,0:T(8,128)S(1)}, f32[32,1024]{1,0:T(8,128)S(1)}, u32[]{:S(2)}, u32[]{:S(2)}) collective-permute-start(f32[32,1024]{1,0:T(8,128)S(1)} %copy-done), channel_id=1, source_target_pairs={{0,4},{2,6},{4,0},{6,2},{1,5},{3,7},{5,1},{7,3},{8,12},{10,14},{12... | collective-permute-start | bytes 393224 | tf_op jit(solution)/shard_map/ppermute | solution.py:267
  41.5 3.1 %collective-permute-start.2 = (f32[32,1024]{1,0:T(8,128)S(1)}, f32[32,1024]{1,0:T(8,128)S(1)}, u32[]{:S(2)}, u32[]{:S(2)}) collective-permute-start(f32[32,1024]{1,0:T(8,128)S(1)} %copy-done), channel_id=1, source_target_pairs={{0,6},{2,0},{4,2},{6,4},{1,7},{3,1},{5,3},{7,5},{8,14},{10,8},{12,... | collective-permute-start | bytes 393224 | tf_op jit(solution)/shard_map/ppermute | solution.py:267
  44.6 0.0 collective-permute-done.refs_7_
  44.6 1.1 %collective-permute-done.1.refs_8_ = f32[32,1024]{1,0:T(8,128)S(1)} collective-permute-done((f32[32,1024]{1,0:T(8,128)S(1)}, f32[32,1024]{1,0:T(8,128)S(1)}, u32[]{:S(2)}, u32[]{:S(2)}) %collective-permute-start.1) | collective-permute-done | bytes 131104 | tf_op jit(solution)/shard_map/ppermute | solution.py:267
  45.8 2.5 %collective-permute-done.2.refs_9_ = f32[32,1024]{1,0:T(8,128)S(1)} collective-permute-done((f32[32,1024]{1,0:T(8,128)S(1)}, f32[32,1024]{1,0:T(8,128)S(1)}, u32[]{:S(2)}, u32[]{:S(2)}) %collective-permute-start.2) | collective-permute-done | bytes 131104 | tf_op jit(solution)/shard_map/ppermute | solution.py:267
  48.3 0.0 all-to-all-done.2.refs_2_
  48.3 0.0 copy-done.3
  48.3 0.0 copy-done.4
  48.3 0.0 copy-done.2
  48.3 0.7 collect.3
  49.0 7.3 %collective-permute-start.3 = (f32[128,1024]{1,0:T(8,128)S(1)}, f32[128,1024]{1,0:T(8,128)S(1)}, u32[]{:S(2)}, u32[]{:S(2)}) collective-permute-start(f32[128,1024]{1,0:T(8,128)S(1)} %get-tuple-element.30.same_ref), channel_id=1, source_target_pairs={{0,1},{1,0},{2,3},{3,2},{4,5},{5,4},{6,7},{7,6},{8,9},{9,8},{10,11... | collective-permute-start | bytes 1572872 | tf_op jit(solution)/shard_map/ppermute | solution.py:294
  57.0 0.0 copy-start.1
  57.0 7.0 %all_to_all.42.recv_ref = f32[4,4,8,128]{3,2,1,0:T(8,128)S(1)} all-to-all(f32[4,4,8,128]{3,2,1,0:T(8,128)S(1)} %get-tuple-element.34), channel_id=1, replica_groups=mesh['z'=16,'y'=4,'x'=4,'core'=2] {'y'}, dimensions={0} | all-to-all | bytes 131072 | tf_op jit(solution)/shard_map/all_to_all | solution.py:296
  64.0 0.0 collective-permute-done.3.other_ref
  64.0 0.0 copy-done.1
  64.0 1.3 %assemble_gram.1 = (f32[32,1024]{1,0:T(8,128)}, f32[2,4,32,32]{3,2,1,0:T(8,128)S(1)}) custom-call(f32[4,4,8,128]{3,2,1,0:T(8,128)S(1)} %all_to_all.42.recv_ref, s32[4,128]{1,0:T(4,128)S(1)} %get-tuple-element.27.rows_ref, f32[4,128]{1,0:T(4,128)S(1)} %get-tuple-element.28.live_ref, f32[32,1024]{1,0:T(8,128)S(1)} %copy-done.1, ...), custom_call_target="tpu_custom_call" | custom-call | tf_op jit(solution)/shard_map/assemble_gram/pallas_call | solution.py:297
  65.2 0.1 all_to_all.34
  65.4 13.2 %all_to_all.43 = f32[32,1,256]{2,1,0:T(1,128)S(1)} all-to-all(f32[32,1,256]{2,1,0:T(1,128)S(1)} %all_to_all.34), channel_id=1, replica_groups=mesh['z'=16,'y'=4,'x'=4,'core'=2] {'y','x','core'}, dimensions={0} | all-to-all | bytes 65536 | tf_op jit(solution)/shard_map/all_to_all | solution.py:311
  78.6 26.3 %all_to_all.44 = f32[128,1,128]{2,1,0:T(1,128)S(1)} all-to-all(f32[128,1,128]{2,1,0:T(1,128)S(1)} %bitcast.30), channel_id=1, replica_groups=mesh['z'=16,'y'=4,'x'=4,'core'=2] {'z','x','core'}, dimensions={0} | all-to-all | bytes 131072 | tf_op jit(solution)/shard_map/all_to_all | solution.py:314
  104.9 0.7 sum_columns.1
  (4 shorter events, 0.0 us)
Async XLA Ops:
  19.0 15.1 %copy-start = (f32[32,1024]{1,0:T(8,128)S(1)}, f32[32,1024]{1,0:T(8,128)}, u32[]{:S(2)}) copy-start(f32[32,1024]{1,0:T(8,128)} %refs_6_.3) | copy-start | bytes 393220
  19.0 29.3 %copy-start.3 = (s32[1,4,128]{2,1,0:T(4,128)S(1)}, s32[1,4,128]{2,1,0:T(4,128)}, u32[]{:S(2)}) copy-start(s32[1,4,128]{2,1,0:T(4,128)} %param.18) | copy-start | bytes 6148
  19.0 29.3 %copy-start.4 = (s32[1,4,128]{2,1,0:T(4,128)S(1)}, s32[1,4,128]{2,1,0:T(4,128)}, u32[]{:S(2)}) copy-start(s32[1,4,128]{2,1,0:T(4,128)} %param.19) | copy-start | bytes 6148
  19.0 29.3 %all-to-all-start.2 = ((f32[64,8,128]{2,1,0:T(8,128)}), f32[64,8,128]{2,1,0:T(8,128)S(1)}, u32[]{:S(2)}, u32[]{:S(2)}) async-start(f32[64,8,128]{2,1,0:T(8,128)} %get-tuple-element.24), calls=%async_computation.2 | async-start | bytes 524288 | tf_op jit(solution)/shard_map/all_to_all | solution.py:240
  34.0 14.3 %copy-start.2 = (s32[1024]{0:T(1024)S(1)}, s32[1024]{0:T(1024)}, u32[]{:S(2)}) copy-start(s32[1024]{0:T(1024)} %param.15) | copy-start | bytes 12292
  34.0 10.6 %collective-permute-start = (f32[32,1024]{1,0:T(8,128)S(1)}, f32[32,1024]{1,0:T(8,128)S(1)}, u32[]{:S(2)}, u32[]{:S(2)}) collective-permute-start(f32[32,1024]{1,0:T(8,128)S(1)} %copy-done), channel_id=1, source_target_pairs={{0,2},{2,4},{4,6},{6,0},{1,3},{3,5},{5,7},{7,1},{8,10},{10,12},{12... | collective-permute-start | bytes 393224 | tf_op jit(solution)/shard_map/ppermute | solution.py:267
  37.2 8.6 %collective-permute-start.1 = (f32[32,1024]{1,0:T(8,128)S(1)}, f32[32,1024]{1,0:T(8,128)S(1)}, u32[]{:S(2)}, u32[]{:S(2)}) collective-permute-start(f32[32,1024]{1,0:T(8,128)S(1)} %copy-done), channel_id=1, source_target_pairs={{0,4},{2,6},{4,0},{6,2},{1,5},{3,7},{5,1},{7,3},{8,12},{10,14},{12... | collective-permute-start | bytes 393224 | tf_op jit(solution)/shard_map/ppermute | solution.py:267
  41.5 6.7 %collective-permute-start.2 = (f32[32,1024]{1,0:T(8,128)S(1)}, f32[32,1024]{1,0:T(8,128)S(1)}, u32[]{:S(2)}, u32[]{:S(2)}) collective-permute-start(f32[32,1024]{1,0:T(8,128)S(1)} %copy-done), channel_id=1, source_target_pairs={{0,6},{2,0},{4,2},{6,4},{1,7},{3,1},{5,3},{7,5},{8,14},{10,8},{12,... | collective-permute-start | bytes 393224 | tf_op jit(solution)/shard_map/ppermute | solution.py:267
  49.0 15.0 %collective-permute-start.3 = (f32[128,1024]{1,0:T(8,128)S(1)}, f32[128,1024]{1,0:T(8,128)S(1)}, u32[]{:S(2)}, u32[]{:S(2)}) collective-permute-start(f32[128,1024]{1,0:T(8,128)S(1)} %get-tuple-element.30.same_ref), channel_id=1, source_target_pairs={{0,1},{1,0},{2,3},{3,2},{4,5},{5,4},{6,7},{7,6},{8,9},{9,8},{10,11... | collective-permute-start | bytes 1572872 | tf_op jit(solution)/shard_map/ppermute | solution.py:294
  57.0 7.0 %copy-start.1 = (f32[32,1024]{1,0:T(8,128)S(1)}, f32[32,1024]{1,0:T(8,128)}, u32[]{:S(2)}) copy-start(f32[32,1024]{1,0:T(8,128)} %get-tuple-element.29.mass_ref) | copy-start | bytes 393220

commit v5 on v4

--- a/solution.py
+++ b/solution.py
@@ -66,18 +66,20 @@
 
     copies[0].wait()
     fill(0)
-    for copy in copies[1:]:
+    fill(1)
+    for copy in copies[1:4]:
         copy.wait()
     snap = snap_ref[...]
     snap2 = split2(snap)
-    fill_one_hot(slot_ref, [jnp.concatenate([rows_ref[k : k + 1, :] for k in range(4)], axis=1)])
-    fill(1)
     for step in range(steps):
         element(step)
         if step > 0:
             add(step - 1)
         if step + 2 < steps:
             fill(step + 2)
+    for copy in copies[4:]:
+        copy.wait()
+    fill_one_hot(slot_ref, [jnp.concatenate([rows_ref[k : k + 1, :] for k in range(4)], axis=1)])
     add(steps - 1)
     diag = acc_ref[2 * snaps : 2 * snaps + 1] + acc_ref[2 * snaps + 8 : 2 * snaps + 9]
     mass = acc_ref[:snaps] + acc_ref[snaps : 2 * snaps] + snap * diag

time: 106 us -> 106 us (level)
  no operation moved by 1% of the time
where the time goes in v5:
time: 106 us
  blocking collectives  56.1 us (53%)
  starting transfers between devices  32.9 us (31%)
  Pallas kernels  11.5 us (11%)
  waiting for transfers between devices  3.67 us (3%)
  between operations  1.4 us (1%)
    all_to_all x1, blocking collectives, per_device(): gram = lax.all_to_all(gram, ('z', 'x', 'core'), 0, 0, tiled=True)  26.3 us
    all_to_all x1, starting transfers between devices, route(): far = lax.all_to_all(send, 'z', 0, 0, tiled=True)  15 us
    all_to_all x1, blocking collectives, per_device(): lax.all_to_all(gram.reshape(ys * groups, per_z * 4 * snaps), ('y', 'x', '...  13.3 us
    ppermute x3, starting transfers between devices, per_device(): lax.ppermute(snapshots, 'x', [(x, (x + away) % xs) for x in range(xs)])  10.5 us
    all_to_all x1, blocking collectives, per_device(): recv = lax.all_to_all(send, 'y', 0, 0, tiled=True)  9.59 us
    pallas_call x1, Pallas kernels, per_device(): pl.pallas_call(local_kernel, out_shape=(jax.ShapeDtypeStruct((snaps, node...  7.76 us
    ppermute x1, starting transfers between devices, per_device(): lax.ppermute(snaps_x, 'core', [(c, (c + 1) % cores) for c in range(cores)])  7.3 us
    all_to_all x1, blocking collectives, per_device(): recv = lax.all_to_all(picked, 'y', 0, 0, tiled=True)  6.99 us
  transfers between devices with their start and end apart: 5, of which 2 were waited for; matrix products, arithmetic and copies ran while one was open for 0% of the time, Pallas kernels for 0%

profile of v5, /device:TPU:1, one launch (start us, length us, event | category | flops | bytes accessed | tf_op | source)
XLA Modules:
  0.0 105.8 jit_solution(5359797399193611227)
XLA Ops:
  0.6 7.8 %local_mass.1 = (f32[32,1024]{1,0:T(8,128)}, f32[4,5,8,128]{3,2,1,0:T(8,128)}) custom-call(s32[4,5120]{1,0:T(4,128)} %refs_0_.2, s32[1,5120]{1,0:T(1,128)} %bitcast.33, f32[1,5120]{1,0:T(1,128)} %bitcast.34, f32[32,1024]{1,0:T(8,128)} %refs_6_.3, s32[4,128]{1,0:T(4,128)} %bitcast.23, s32[4,128]{1,0:T(4,128)} %bitcast.25, s32[1,4]{1,0:T(1,128)} %refs_6_.2, ...), custom_call_target="tpu_custom_call" | custom-call | flops 10000000000 | bytes 1000000 | tf_op jit(solution)/shard_map/local_mass/pallas_call | solution.py:272
  8.4 9.6 %all_to_all.41.refs_0_ = f32[4,5,8,128]{3,2,1,0:T(8,128)S(1)} all-to-all(f32[4,5,8,128]{3,2,1,0:T(8,128)} %get-tuple-element.22), channel_id=1, replica_groups=mesh['z'=16,'y'=4,'x'=4,'core'=2] {'y'}, dimensions={0} | all-to-all | bytes 163840 | tf_op jit(solution)/shard_map/all_to_all | solution.py:291
  18.0 1.1 %spread.3 = (f32[64,8,128]{2,1,0:T(8,128)}, s32[16,128]{1,0:T(8,128)S(1)}) custom-call(f32[4,5,8,128]{3,2,1,0:T(8,128)S(1)} %all_to_all.41.refs_0_), custom_call_target="tpu_custom_call" | custom-call | tf_op jit(solution)/shard_map/spread/pallas_call | solution.py:234
  19.1 0.0 copy-start
  19.1 0.0 copy-start.3
  19.1 0.0 copy-start.4
  19.1 15.0 %all-to-all-start.2 = ((f32[64,8,128]{2,1,0:T(8,128)}), f32[64,8,128]{2,1,0:T(8,128)S(1)}, u32[]{:S(2)}, u32[]{:S(2)}) async-start(f32[64,8,128]{2,1,0:T(8,128)} %get-tuple-element.24), calls=%async_computation.2 | async-start | bytes 524288 | tf_op jit(solution)/shard_map/all_to_all | solution.py:242
  34.2 0.0 copy-done
  34.2 0.0 copy-start.2
  34.2 3.1 %collective-permute-start = (f32[32,1024]{1,0:T(8,128)S(1)}, f32[32,1024]{1,0:T(8,128)S(1)}, u32[]{:S(2)}, u32[]{:S(2)}) collective-permute-start(f32[32,1024]{1,0:T(8,128)S(1)} %copy-done), channel_id=1, source_target_pairs={{0,2},{2,4},{4,6},{6,0},{1,3},{3,5},{5,7},{7,1},{8,10},{10,12},{12... | collective-permute-start | bytes 393224 | tf_op jit(solution)/shard_map/ppermute | solution.py:269
  37.3 4.4 %collective-permute-start.1 = (f32[32,1024]{1,0:T(8,128)S(1)}, f32[32,1024]{1,0:T(8,128)S(1)}, u32[]{:S(2)}, u32[]{:S(2)}) collective-permute-start(f32[32,1024]{1,0:T(8,128)S(1)} %copy-done), channel_id=1, source_target_pairs={{0,4},{2,6},{4,0},{6,2},{1,5},{3,7},{5,1},{7,3},{8,12},{10,14},{12... | collective-permute-start | bytes 393224 | tf_op jit(solution)/shard_map/ppermute | solution.py:269
  41.7 3.1 %collective-permute-start.2 = (f32[32,1024]{1,0:T(8,128)S(1)}, f32[32,1024]{1,0:T(8,128)S(1)}, u32[]{:S(2)}, u32[]{:S(2)}) collective-permute-start(f32[32,1024]{1,0:T(8,128)S(1)} %copy-done), channel_id=1, source_target_pairs={{0,6},{2,0},{4,2},{6,4},{1,7},{3,1},{5,3},{7,5},{8,14},{10,8},{12,... | collective-permute-start | bytes 393224 | tf_op jit(solution)/shard_map/ppermute | solution.py:269
  44.8 0.0 collective-permute-done.refs_7_
  44.8 1.1 %collective-permute-done.1.refs_8_ = f32[32,1024]{1,0:T(8,128)S(1)} collective-permute-done((f32[32,1024]{1,0:T(8,128)S(1)}, f32[32,1024]{1,0:T(8,128)S(1)}, u32[]{:S(2)}, u32[]{:S(2)}) %collective-permute-start.1) | collective-permute-done | bytes 131104 | tf_op jit(solution)/shard_map/ppermute | solution.py:269
  45.9 2.5 %collective-permute-done.2.refs_9_ = f32[32,1024]{1,0:T(8,128)S(1)} collective-permute-done((f32[32,1024]{1,0:T(8,128)S(1)}, f32[32,1024]{1,0:T(8,128)S(1)}, u32[]{:S(2)}, u32[]{:S(2)}) %collective-permute-start.2) | collective-permute-done | bytes 131104 | tf_op jit(solution)/shard_map/ppermute | solution.py:269
  48.5 0.0 all-to-all-done.2.refs_2_
  48.5 0.0 copy-done.3
  48.5 0.0 copy-done.4
  48.5 0.0 copy-done.2
  48.5 0.7 collect.3
  49.2 7.3 %collective-permute-start.3 = (f32[128,1024]{1,0:T(8,128)S(1)}, f32[128,1024]{1,0:T(8,128)S(1)}, u32[]{:S(2)}, u32[]{:S(2)}) collective-permute-start(f32[128,1024]{1,0:T(8,128)S(1)} %get-tuple-element.30.same_ref), channel_id=1, source_target_pairs={{0,1},{1,0},{2,3},{3,2},{4,5},{5,4},{6,7},{7,6},{8,9},{9,8},{10,11... | collective-permute-start | bytes 1572872 | tf_op jit(solution)/shard_map/ppermute | solution.py:296
  57.1 0.0 copy-start.1
  57.1 7.0 %all_to_all.42.recv_ref = f32[4,4,8,128]{3,2,1,0:T(8,128)S(1)} all-to-all(f32[4,4,8,128]{3,2,1,0:T(8,128)S(1)} %get-tuple-element.34), channel_id=1, replica_groups=mesh['z'=16,'y'=4,'x'=4,'core'=2] {'y'}, dimensions={0} | all-to-all | bytes 131072 | tf_op jit(solution)/shard_map/all_to_all | solution.py:298
  64.1 0.0 collective-permute-done.3.other_ref
  64.1 0.0 copy-done.1
  64.1 1.3 %assemble_gram.1 = (f32[32,1024]{1,0:T(8,128)}, f32[2,4,32,32]{3,2,1,0:T(8,128)S(1)}) custom-call(f32[4,4,8,128]{3,2,1,0:T(8,128)S(1)} %all_to_all.42.recv_ref, s32[4,128]{1,0:T(4,128)S(1)} %get-tuple-element.27.rows_ref, f32[4,128]{1,0:T(4,128)S(1)} %get-tuple-element.28.live_ref, f32[32,1024]{1,0:T(8,128)S(1)} %copy-done.1, ...), custom_call_target="tpu_custom_call" | custom-call | tf_op jit(solution)/shard_map/assemble_gram/pallas_call | solution.py:299
  65.4 0.1 all_to_all.34
  65.6 13.3 %all_to_all.43 = f32[32,1,256]{2,1,0:T(1,128)S(1)} all-to-all(f32[32,1,256]{2,1,0:T(1,128)S(1)} %all_to_all.34), channel_id=1, replica_groups=mesh['z'=16,'y'=4,'x'=4,'core'=2] {'y','x','core'}, dimensions={0} | all-to-all | bytes 65536 | tf_op jit(solution)/shard_map/all_to_all | solution.py:313
  78.8 26.3 %all_to_all.44 = f32[128,1,128]{2,1,0:T(1,128)S(1)} all-to-all(f32[128,1,128]{2,1,0:T(1,128)S(1)} %bitcast.30), channel_id=1, replica_groups=mesh['z'=16,'y'=4,'x'=4,'core'=2] {'z','x','core'}, dimensions={0} | all-to-all | bytes 131072 | tf_op jit(solution)/shard_map/all_to_all | solution.py:316
  105.1 0.7 sum_columns.1
  (4 shorter events, 0.0 us)
Async XLA Ops:
  19.1 15.1 %copy-start = (f32[32,1024]{1,0:T(8,128)S(1)}, f32[32,1024]{1,0:T(8,128)}, u32[]{:S(2)}) copy-start(f32[32,1024]{1,0:T(8,128)} %refs_6_.3) | copy-start | bytes 393220
  19.1 29.3 %copy-start.3 = (s32[1,4,128]{2,1,0:T(4,128)S(1)}, s32[1,4,128]{2,1,0:T(4,128)}, u32[]{:S(2)}) copy-start(s32[1,4,128]{2,1,0:T(4,128)} %param.18) | copy-start | bytes 6148
  19.1 29.3 %copy-start.4 = (s32[1,4,128]{2,1,0:T(4,128)S(1)}, s32[1,4,128]{2,1,0:T(4,128)}, u32[]{:S(2)}) copy-start(s32[1,4,128]{2,1,0:T(4,128)} %param.19) | copy-start | bytes 6148
  19.1 29.3 %all-to-all-start.2 = ((f32[64,8,128]{2,1,0:T(8,128)}), f32[64,8,128]{2,1,0:T(8,128)S(1)}, u32[]{:S(2)}, u32[]{:S(2)}) async-start(f32[64,8,128]{2,1,0:T(8,128)} %get-tuple-element.24), calls=%async_computation.2 | async-start | bytes 524288 | tf_op jit(solution)/shard_map/all_to_all | solution.py:242
  34.2 14.3 %copy-start.2 = (s32[1024]{0:T(1024)S(1)}, s32[1024]{0:T(1024)}, u32[]{:S(2)}) copy-start(s32[1024]{0:T(1024)} %param.15) | copy-start | bytes 12292
  34.2 10.6 %collective-permute-start = (f32[32,1024]{1,0:T(8,128)S(1)}, f32[32,1024]{1,0:T(8,128)S(1)}, u32[]{:S(2)}, u32[]{:S(2)}) collective-permute-start(f32[32,1024]{1,0:T(8,128)S(1)} %copy-done), channel_id=1, source_target_pairs={{0,2},{2,4},{4,6},{6,0},{1,3},{3,5},{5,7},{7,1},{8,10},{10,12},{12... | collective-permute-start | bytes 393224 | tf_op jit(solution)/shard_map/ppermute | solution.py:269
  37.3 8.6 %collective-permute-start.1 = (f32[32,1024]{1,0:T(8,128)S(1)}, f32[32,1024]{1,0:T(8,128)S(1)}, u32[]{:S(2)}, u32[]{:S(2)}) collective-permute-start(f32[32,1024]{1,0:T(8,128)S(1)} %copy-done), channel_id=1, source_target_pairs={{0,4},{2,6},{4,0},{6,2},{1,5},{3,7},{5,1},{7,3},{8,12},{10,14},{12... | collective-permute-start | bytes 393224 | tf_op jit(solution)/shard_map/ppermute | solution.py:269
  41.7 6.7 %collective-permute-start.2 = (f32[32,1024]{1,0:T(8,128)S(1)}, f32[32,1024]{1,0:T(8,128)S(1)}, u32[]{:S(2)}, u32[]{:S(2)}) collective-permute-start(f32[32,1024]{1,0:T(8,128)S(1)} %copy-done), channel_id=1, source_target_pairs={{0,6},{2,0},{4,2},{6,4},{1,7},{3,1},{5,3},{7,5},{8,14},{10,8},{12,... | collective-permute-start | bytes 393224 | tf_op jit(solution)/shard_map/ppermute | solution.py:269
  49.2 15.0 %collective-permute-start.3 = (f32[128,1024]{1,0:T(8,128)S(1)}, f32[128,1024]{1,0:T(8,128)S(1)}, u32[]{:S(2)}, u32[]{:S(2)}) collective-permute-start(f32[128,1024]{1,0:T(8,128)S(1)} %get-tuple-element.30.same_ref), channel_id=1, source_target_pairs={{0,1},{1,0},{2,3},{3,2},{4,5},{5,4},{6,7},{7,6},{8,9},{9,8},{10,11... | collective-permute-start | bytes 1572872 | tf_op jit(solution)/shard_map/ppermute | solution.py:296
  57.1 7.0 %copy-start.1 = (f32[32,1024]{1,0:T(8,128)S(1)}, f32[32,1024]{1,0:T(8,128)}, u32[]{:S(2)}) copy-start(f32[32,1024]{1,0:T(8,128)} %get-tuple-element.29.mass_ref) | copy-start | bytes 393220
